TPU v7x, 32 devices: a whole 2x2x4 slice. The times are simulated.
32 devices in a mesh: grp: 2 (over x), view: 16 (over z, y, core).
Axes of the slice: x: 2, y: 2, z: 4, core: 2. Of those that a mesh axis runs over, the one named last changes fastest.
Arguments:
- volume: float32 [64, 16, 2, 512], P(('grp', 'view')), may hold values from 0 to 2
- footprint: bfloat16 [64, 2, 512, 896], P(('grp', 'view')), may hold values from -0.1875 to 0.1875
- measured: bfloat16 [256, 64, 896], P(('grp', 'view')), may hold values from 0 to 3
- angle_index: int32 [256], P(('grp', 'view')), may hold values from 0 to 1
- cover: int32 [256, 4], P(('grp', 'view')), may hold values from 0 to 63, as said below
- offset: int32 [256, 4], P(('grp', 'view')), may hold values from 0 to 48
- count: int32 [256], P(('grp', 'view')), may hold values from 1 to 4
Outputs:
- gradient: float32 [64, 16, 2, 512], P(('grp', 'view'))
Inputs may be any that keep to these rules, and one draw needn't show every extreme that they name: Let p = v // 8. cover[v,k] lies between max(p - 4, 0) * 2 and min(p + 5, 32) * 2 - 1, and both ends are named by some slot 0 of p's views.
All inputs are finite; a program needn't handle non-finite values.
Results may differ from a plain program's by a relative error of at most 0.0019.
Values may be sent and summed in bfloat16 or wider, within the bound.
No kernel may reach another device: no remote copies, remote signals or barrier semaphores. Data moves between devices by JAX's collectives and lax.ppermute only.
A program may use at most 64 MiB of HBM per device.

v0:
```python
import functools

import jax
import jax.numpy as jnp
from jax import lax
from jax.experimental import pallas as pl
from jax.experimental.pallas import tpu as pltpu
from jax.sharding import PartitionSpec as P

AXES = ("grp", "view")
STATIC = 12
MORE = 4
DELTA = 0.5
PRIOR_WEIGHT = 2.0


def both_ways(pairs):
    return pairs + [(b, a) for a, b in pairs]


def exchange_pairs(devices):
    chips = devices // 2
    swap = [(i, i ^ 1) for i in range(devices)]
    edge_y = [(i, i + 1) for i in range(0, chips, 2)]
    edge_d = [(i, i + 1) for i in range(1, chips - 1, 2)]
    edge_a = [(i + j, i + j + 2) for i in range(0, chips, 4) for j in (0, 1)]
    edge_b = [(i + j, i + j + 2) for i in range(2, chips - 2, 4) for j in (0, 1)]
    idle = [(0, 1), (chips - 2, chips - 1)]
    on_core = lambda edges, core: [(2 * a + core, 2 * b + core) for a, b in edges]
    last = devices - 1
    ends = [(0, 4), (4, 1), (1, 0), (last - 1, last - 5), (last - 5, last), (last, last - 1)]
    first = both_ways(on_core(edge_a[1:-1], 0) + on_core(edge_d, 1)) + ends
    second = both_ways(on_core(edge_b + idle, 0) + on_core(edge_y, 1))
    return swap, first, second


def load_kernel(source, target, own_ref, sem):
    copy = pltpu.make_async_copy(source, target, sem)
    copy.start()
    copy.wait()
    strip, row = target.shape[1:]
    for y in range(strip):
        own_ref[:, y * row : (y + 1) * row] = target[:, y, :].astype(jnp.bfloat16)


def join_kernel(mine_ref, own_ref, other_ref, first_ref, second_ref, *, here):
    slices, strip, row = other_ref.shape
    tiles = strip * row // 128
    part = slices
    rest = {}
    for name, ref in (("mine", mine_ref), ("other", other_ref)):
        for at in (0, slices - 1):
            for y in range(strip):
                whole = ref[at : at + 1, y, :]
                left = whole - whole.astype(jnp.bfloat16).astype(jnp.float32)
                mid = left.astype(jnp.bfloat16).astype(jnp.float32)
                rest[name, at, y] = (mid, left - mid)
    position = here()
    core = lax.rem(position, 2)
    odd = lax.rem(position // 2, 2)
    for y in range(strip):
        packed = other_ref[:, y, :].astype(jnp.bfloat16)
        for k in range(row // 128):
            tile = y * (row // 128) + k
            cols = slice(k * 128, (k + 1) * 128)
            for ref in (first_ref, second_ref):
                ref[tile * 2 * part : tile * 2 * part + part, :] = own_ref[
                    :, tile * 128 : (tile + 1) * 128
                ]
                ref[tile * 2 * part + part : (tile + 1) * 2 * part, :] = packed[:, cols]
    top, bottom = [], []
    for y in range(strip):
        for k in range(row // 128):
            cols = slice(k * 128, (k + 1) * 128)
            for which in range(2):
                a = rest["mine", 0, y][which][:, cols]
                b = rest["other", 0, y][which][:, cols]
                top.append(jnp.where(core == 0, a, b))
                a = rest["mine", slices - 1, y][which][:, cols]
                b = rest["other", slices - 1, y][which][:, cols]
                bottom.append(jnp.where(core == 1, a, b))
    top = jnp.concatenate(top, axis=0)
    bottom = jnp.concatenate(bottom, axis=0)
    tail = slice(tiles * 2 * part, tiles * 2 * part + 2 * tiles)
    first_ref[tail, :] = jnp.where(odd == 1, bottom, top).astype(jnp.bfloat16)
    second_ref[tail, :] = jnp.where(odd == 1, top, bottom).astype(jnp.bfloat16)


def unfold(ref, begin, window, first_row, piece):
    for j in range(window.shape[1] // 128):
        window[first_row : first_row + piece, j * 128 : (j + 1) * 128] = ref[
            begin + j * piece : begin + (j + 1) * piece, :
        ]


def window_rows(block, position, chips, local_blocks, slab):
    part = local_blocks * slab
    piece = 2 * part
    core = lax.rem(position, 2)
    chip = position // 2
    owner = block // local_blocks
    owner_core = lax.rem(owner, 2)
    delta = owner // 2 - chip
    flag = lambda what: jnp.where(what, 1, 0)
    up = flag(delta > 0)
    nearer = jnp.abs(delta) == 1
    is_y = flag(up == 1 - lax.rem(chip, 2))
    is_a = flag(up == flag(lax.rem(chip, 4) < 2))
    second = jnp.where(nearer, is_y, 1 - is_a)
    via = flag(nearer)
    end = flag((chip == 0) | (chip == chips - 1))
    held = jnp.where(nearer, 1, is_a * end)
    away = (2 * jnp.abs(held - core) + second) * piece + jnp.abs(owner_core - via) * part
    here = 4 * piece + jnp.abs(owner_core - core) * part
    return jnp.where(delta == 0, here, away) + lax.rem(block, local_blocks) * slab


class Pairs:
    ROWS = 8
    GROUPS = 3

    def __init__(self, ref, first=0):
        self.ref = ref
        self.first = first

    def each(self, do):
        def body(i, carry):
            do(*(self.ref[self.first + k, i] for k in range(4)))
            return carry

        lax.fori_loop(0, self.ref[self.first + 5, 0], body, 0)

    def gathered(self):
        return self.ref[self.first + 5, 1]

    def target(self, i):
        return self.ref[self.first + 4, i]


def list_pairs(scal, lists, seen, height, held, near_rows, det_rows, tables, slab):
    slots = (scal.shape[0] - 2) // 2
    most = held.shape[1]
    fields, groups = Pairs.ROWS, Pairs.GROUPS

    def clear(i, carry):
        height[i] = jnp.int32(0)
        for table in range(tables):
            seen[i, table] = jnp.int32(0)
        return carry

    lax.fori_loop(0, height.shape[0], clear, 0)
    for k in range(groups):
        lists[fields * k + 5, 0] = jnp.int32(0)
        lists[fields * k + 5, 1] = jnp.int32(0)

    def body(view, carry):
        count = scal[2 * slots, view]
        table = scal[2 * slots + 1, view]
        for slot in range(slots):

            @pl.when(slot < count)
            def _():
                row = scal[slot, view]
                block = row // slab
                group = jnp.minimum(row // near_rows, groups - 1)
                local = row - group * near_rows
                first = fields * group
                at = lists[first + 5, 0]
                used = lists[first + 5, 1]
                rank = seen[block, table]
                top = height[block]
                fresh = rank >= top
                mine = jnp.where(fresh, used, held[block, rank])
                held[block, rank] = mine
                seen[block, table] = rank + 1
                height[block] = jnp.where(fresh, rank + 1, top)
                lists[first, at] = view * det_rows + scal[slots + slot, view]
                lists[first + 1, at] = table
                lists[first + 2, at] = local
                lists[first + 3, at] = mine * slab
                lists[first + 4, mine] = local
                lists[first + 5, 0] = at + 1
                lists[first + 5, 1] = used + jnp.where(fresh, 1, 0)

        return carry

    lax.fori_loop(0, scal.shape[1], body, 0)


def place(pairs, sino, proj, slab):
    width = sino.shape[0] * 128

    def add(target, table, local, dest):
        source = pl.ds(pl.multiple_of(local, slab), slab)
        for tile in range(sino.shape[0]):
            cols = pl.ds(pl.multiple_of(table * width + tile * 128, 128), 128)
            sino[tile, pl.ds(target, slab), :] += proj[source, cols]

    pairs.each(add)


def clear_rows(picked, static_rows):
    picked[0:static_rows, :] = jnp.zeros((static_rows, picked.shape[1]), picked.dtype)


def gather(pairs, sino, decay, picked, static_rows, slab):
    width = sino.shape[0] * 128
    chunk = MORE * slab

    def clear(i, carry):
        here = pl.ds(pl.multiple_of(static_rows + i * chunk, chunk), chunk)
        picked[here, :] = jnp.zeros((chunk, picked.shape[1]), picked.dtype)
        return carry

    more = pairs.gathered() * slab - static_rows
    lax.fori_loop(0, (more + chunk - 1) // chunk, clear, 0)

    def take(source, table, local, dest):
        target = pl.ds(pl.multiple_of(dest, slab), slab)
        here = pl.ds(source, slab)
        for tile in range(sino.shape[0]):
            cols = pl.ds(pl.multiple_of(table * width + tile * 128, 128), 128)
            value = decay[tile, here, :] * sino[tile, here, :]
            picked[target, cols] = value.astype(jnp.bfloat16)

    pairs.each(take)


def back_project(pairs, picked, turned_ref, spread, out_ref, slab):
    static_rows = spread.shape[0]
    static = static_rows // slab
    blocks = pairs.gathered()
    out_ref[...] = jnp.zeros_like(out_ref)

    def add_from(begin):
        def add(i, carry):
            target = pl.ds(pl.multiple_of(pairs.target(i), slab), slab)
            source = pl.ds(pl.multiple_of((i - begin) * slab, slab), slab)
            out_ref[target, :] += spread[source, :]
            return carry

        return add

    spread[...] = jnp.dot(
        picked[0:static_rows, :], turned_ref[...], preferred_element_type=jnp.float32
    )
    lax.fori_loop(0, jnp.minimum(blocks, static), add_from(0), 0)

    def further(c, carry):
        begin = static + c * MORE
        here = pl.ds(pl.multiple_of(begin * slab, MORE * slab), MORE * slab)
        spread[0 : MORE * slab, :] = jnp.dot(
            picked[here, :], turned_ref[...], preferred_element_type=jnp.float32
        )
        lax.fori_loop(begin, jnp.minimum(blocks, begin + MORE), add_from(begin), 0)
        return carry

    lax.fori_loop(0, (blocks - static + MORE - 1) // MORE, further, 0)


def early_kernel(
    both_ref,
    table_hbm,
    measured_hbm,
    cover_hbm,
    offset_hbm,
    count_hbm,
    angle_hbm,
    table_ref,
    turned_ref,
    lists_ref,
    sino_ref,
    decay_ref,
    measured,
    cover,
    offset,
    count,
    angle,
    index,
    scal,
    lists,
    seen,
    height,
    held,
    window,
    proj,
    sems,
    *,
    piece,
    chips,
    local_blocks,
    slab,
    here,
):
    views, det_rows, channels = measured.shape
    slots = cover.shape[0]
    tables = table_hbm.shape[0]
    small = [(cover_hbm, cover), (offset_hbm, offset), (count_hbm, count), (angle_hbm, angle)]
    unfold(both_ref, 0, window, 0, piece)
    copies = [pltpu.make_async_copy(a, b, sems.at[i]) for i, (a, b) in enumerate(small)]
    copies.append(pltpu.make_async_copy(measured_hbm, measured, sems.at[4]))
    for table in range(tables):
        to = table_ref.at[:, table * channels : (table + 1) * channels]
        copies.append(pltpu.make_async_copy(table_hbm.at[table], to, sems.at[5 + table]))
    for copy in copies:
        copy.start()
    for copy in copies[:4]:
        copy.wait()
    index[0:slots, :] = window_rows(cover[...], here(), chips, local_blocks, slab)
    index[slots : 2 * slots, :] = offset[...]
    index[2 * slots : 2 * slots + 1, :] = count[...]
    index[2 * slots + 1 : 2 * slots + 2, :] = angle[...]
    load = fetch(index, scal, sems.at[0])
    copies[4].wait()

    def fade(view, carry):
        rows = pl.ds(pl.multiple_of(view * det_rows, det_rows), det_rows)
        for tile in range(sino_ref.shape[0]):
            value = measured[view, :, tile * 128 : (tile + 1) * 128].astype(jnp.float32)
            decay_ref[tile, rows, :] = jnp.exp(-value)
            sino_ref[tile, rows, :] = -value
        return carry

    lax.fori_loop(0, views, fade, 0)
    load.wait()
    list_pairs(scal, lists, seen, height, held, 2 * piece, det_rows, tables, slab)
    save = fetch(lists, lists_ref, sems.at[0])
    for table in range(tables):
        copies[5 + table].wait()
        cols = slice(table * channels, (table + 1) * channels)
        turned_ref[cols, :] = table_ref[:, cols].T
    proj[...] = jnp.dot(window[...], table_ref[...], preferred_element_type=jnp.float32)
    place(Pairs(lists, 2 * Pairs.ROWS), sino_ref, proj, slab)
    save.wait()


def fetch_group(lists_ref, group, lists, sem):
    return fetch(lists_ref.at[pl.ds(group * Pairs.ROWS, Pairs.ROWS)], lists, sem)


def fetch(source, target, sem):
    load = pltpu.make_async_copy(source, target, sem)
    load.start()
    return load


def project(load, lists, window, table_ref, begun_ref, sino_ref, proj, slab):
    sino_ref[...] = begun_ref[...]
    proj[...] = jnp.dot(window[...], table_ref[...], preferred_element_type=jnp.float32)
    load.wait()
    place(Pairs(lists), sino_ref, proj, slab)


def middle_kernel(
    lists_ref, first_ref, second_ref, table_ref, begun_ref, sino_ref, lists, window, proj, sem, *, slab
):
    load = fetch_group(lists_ref, 0, lists, sem)
    piece = proj.shape[0] // 2
    for k, ref in enumerate((first_ref, second_ref)):
        unfold(ref, 0, window, k * piece, piece)
    project(load, lists, window, table_ref, begun_ref, sino_ref, proj, slab)


def main_kernel(
    lists_ref,
    far_ref,
    table_ref,
    turned_ref,
    begun_ref,
    decay_ref,
    sino_ref,
    give_ref,
    lists,
    window,
    proj,
    picked,
    spread,
    sem,
    *,
    slab,
):
    load = fetch_group(lists_ref, 1, lists, sem)
    clear_rows(picked, spread.shape[0])
    piece = proj.shape[0] // 2
    for k in range(2):
        unfold(far_ref, k * far_ref.shape[0] // 2, window, k * piece, piece)
    project(load, lists, window, table_ref, begun_ref, sino_ref, proj, slab)
    pairs = Pairs(lists)
    gather(pairs, sino_ref, decay_ref, picked, spread.shape[0], slab)
    back_project(pairs, picked, turned_ref, spread, give_ref, slab)


def rest_kernel(
    lists_ref, turned_ref, sino_ref, decay_ref, out_ref, lists, picked, spread, sem, *, group, slab
):
    load = fetch_group(lists_ref, group, lists, sem)
    clear_rows(picked, spread.shape[0])
    load.wait()
    pairs = Pairs(lists)
    gather(pairs, sino_ref, decay_ref, picked, spread.shape[0], slab)
    back_project(pairs, picked, turned_ref, spread, out_ref, slab)


def prior_kernel(
    vol_ref, other_ref, first_ref, second_ref, far_ref, out_ref, *, devices, here
):
    slices, strip, row = vol_ref.shape
    part = slices
    piece = 2 * part
    position = here()
    core = lax.rem(position, 2)
    odd = lax.rem(position // 2, 2)

    def chip_slice(ref, which, base=0):
        at = part if which == 0 else part - 1
        tiles = strip * row // 128

        def column(tile):
            whole = ref[base + tile * piece + at : base + tile * piece + at + 1, :]
            tail = base + tiles * piece + 2 * tile
            mid, low = ref[tail : tail + 1, :], ref[tail + 1 : tail + 2, :]
            return whole.astype(jnp.float32) + (mid.astype(jnp.float32) + low.astype(jnp.float32))

        here = row // 128
        return lambda y: jnp.concatenate([column(y * here + k) for k in range(here)], axis=1)

    def core_slice(which):
        at = (part - 1) * which
        return lambda y: other_ref[at : at + 1, y, :]

    def emit(low, high):
        for y in range(strip):
            cols = slice(y * row, (y + 1) * row)
            here = vol_ref[:, y, :]
            below = jnp.concatenate([low(y), here[:-1]], axis=0)
            above = jnp.concatenate([here[1:], high(y)], axis=0)
            level = lax.broadcasted_iota(jnp.int32, here.shape, 0)
            down = jnp.clip(here - below, -DELTA, DELTA)
            total = jnp.where((level > 0) | (position > 0), down, 0.0)
            up = jnp.clip(here - above, -DELTA, DELTA)
            total += jnp.where((level < slices - 1) | (position < devices - 1), up, 0.0)
            if y > 0:
                total += jnp.clip(here - vol_ref[:, y - 1, :], -DELTA, DELTA)
            if y + 1 < strip:
                total += jnp.clip(here - vol_ref[:, y + 1, :], -DELTA, DELTA)
            lane = lax.broadcasted_iota(jnp.int32, here.shape, 1)
            left = jnp.clip(here - pltpu.roll(here, 1, 1), -DELTA, DELTA)
            total += jnp.where(lane > 0, left, 0.0)
            right = jnp.clip(here - pltpu.roll(here, row - 1, 1), -DELTA, DELTA)
            total += jnp.where(lane < row - 1, right, 0.0)
            out_ref[:, cols] = PRIOR_WEIGHT * total

    @pl.when((core == 0) & (odd == 0))
    def _():
        emit(chip_slice(far_ref, 1), core_slice(0))

    @pl.when((core == 0) & (odd == 1))
    def _():
        emit(chip_slice(far_ref, 1, far_ref.shape[0] // 2), core_slice(0))

    @pl.when((core == 1) & (odd == 0))
    def _():
        emit(core_slice(1), chip_slice(second_ref, 0))

    @pl.when((core == 1) & (odd == 1))
    def _():
        emit(core_slice(1), chip_slice(first_ref, 0))


def last_kernel(arrived_ref, passed_ref, prior_ref, out_hbm, total, sems):
    part, strip, row = total.shape
    copies = []
    step = part // sems.shape[0]
    for k in range(sems.shape[0]):
        here = slice(k * step, (k + 1) * step)
        for y in range(strip):
            cols = slice(y * row, (y + 1) * row)
            total[here, y, :] = (arrived_ref[here, cols] + passed_ref[here, cols]) + prior_ref[
                here, cols
            ]
        copies.append(pltpu.make_async_copy(total.at[here], out_hbm.at[here], sems.at[k]))
        copies[-1].start()
    for copy in copies:
        copy.wait()


def shards(volume, footprint, measured, angle_index, cover, offset, count):
    local_blocks, slab, strip, row = volume.shape
    views, det_rows, channels = measured.shape
    tables = footprint.shape[0]
    slots = cover.shape[1]
    plane = strip * row
    devices = lax.axis_size(AXES)
    position = lax.axis_index(AXES)
    swap, first, second = exchange_pairs(devices)
    back = lambda pairs: [(b, a) for a, b in pairs]
    send = lambda value, pairs: lax.ppermute(value, AXES, pairs)
    part = local_blocks * slab
    piece = 2 * part
    flat = volume.reshape(part, strip, row)
    table = footprint.reshape(tables, plane, channels)
    vmem = pl.BlockSpec(memory_space=pltpu.VMEM)
    smem = pl.BlockSpec(memory_space=pltpu.SMEM)
    shape = jax.ShapeDtypeStruct
    room = lambda mib: pltpu.CompilerParams(vmem_limit_bytes=mib * 1024 * 1024)
    cost = lambda flops, size: pl.CostEstimate(flops=flops, bytes_accessed=size, transcendentals=0)

    here = lambda: lax.axis_index("grp") * lax.axis_size("view") + lax.axis_index("view")
    hbm = pl.BlockSpec(memory_space=pltpu.HBM)
    stay = lambda value: pltpu.with_memory_space_constraint(value, pltpu.HBM)

    other = send(flat, swap)
    mine, packed = pl.pallas_call(
        load_kernel,
        out_shape=(shape(flat.shape, flat.dtype), shape((part, plane), jnp.bfloat16)),
        in_specs=[hbm],
        out_specs=(vmem, vmem),
        scratch_shapes=[pltpu.SemaphoreType.DMA],
        compiler_params=room(4),
        cost_estimate=cost(1, 1),
        name="load",
    )(stay(flat))
    other, mine, packed = lax.optimization_barrier((other, mine, packed))
    sent = shape((plane // 128 * (piece + 2), 128), jnp.bfloat16)
    for_first, for_second = pl.pallas_call(
        functools.partial(join_kernel, here=here),
        out_shape=(sent, sent),
        in_specs=[vmem] * 3,
        out_specs=(vmem, vmem),
        compiler_params=room(4),
        name="join",
    )(mine, packed, other)
    got_second = send(for_second, second)
    got_first = send(for_first, first)

    sino_shape = shape((channels // 128, views * det_rows, 128), jnp.float32)
    lists_shape = (Pairs.ROWS * Pairs.GROUPS, views * slots)
    table_vmem, turned, lists, sino, decay = pl.pallas_call(
        functools.partial(
            early_kernel,
            piece=piece,
            chips=devices // 2,
            local_blocks=local_blocks,
            slab=slab,
            here=here,
        ),
        out_shape=(
            shape((plane, tables * channels), table.dtype),
            shape((tables * channels, plane), table.dtype),
            shape(lists_shape, jnp.int32),
            sino_shape,
            sino_shape,
        ),
        in_specs=[vmem] + [hbm] * 6,
        out_specs=(vmem,) * 5,
        scratch_shapes=[
            pltpu.VMEM(measured.shape, measured.dtype),
            pltpu.VMEM((slots, views), jnp.int32),
            pltpu.VMEM((slots, views), jnp.int32),
            pltpu.VMEM((1, views), jnp.int32),
            pltpu.VMEM((1, views), jnp.int32),
            pltpu.VMEM((2 * slots + 2, views), jnp.int32),
            pltpu.SMEM((2 * slots + 2, views), jnp.int32),
            pltpu.SMEM(lists_shape, jnp.int32),
            pltpu.SMEM((5 * piece // slab, tables), jnp.int32),
            pltpu.SMEM((5 * piece // slab,), jnp.int32),
            pltpu.SMEM((5 * piece // slab, views * slots), jnp.int32),
            pltpu.VMEM((piece, plane), jnp.bfloat16),
            pltpu.VMEM((piece, tables * channels), jnp.float32),
            pltpu.SemaphoreType.DMA((5 + tables,)),
        ],
        compiler_params=room(16),
        cost_estimate=cost(1, 1),
        name="early",
    )(
        for_second,
        stay(table),
        stay(measured),
        stay(cover.T),
        stay(offset.T),
        stay(count.reshape(1, views)),
        stay(angle_index.reshape(1, views)),
    )
    got_second, got_first, table_vmem, turned, lists, sino, decay = lax.optimization_barrier(
        (got_second, got_first, table_vmem, turned, lists, sino, decay)
    )
    index = [pltpu.SMEM((Pairs.ROWS, views * slots), jnp.int32)]
    waits = [pltpu.SemaphoreType.DMA]
    rows_of = lambda rows: [pltpu.VMEM((rows, tables * channels), jnp.float32)]
    window = [pltpu.VMEM((2 * piece, plane), jnp.bfloat16)]
    picks_of = lambda blocks: [
        pltpu.VMEM(((max(views * slots, blocks) + MORE) * slab, tables * channels), jnp.bfloat16),
        pltpu.VMEM((blocks * slab, plane), jnp.float32),
    ]

    far = send(jnp.concatenate([got_first, got_second], axis=0), swap)
    sino = pl.pallas_call(
        functools.partial(middle_kernel, slab=slab),
        out_shape=sino_shape,
        in_specs=[vmem] * 5,
        out_specs=vmem,
        scratch_shapes=index + window + rows_of(2 * piece) + waits,
        compiler_params=room(16),
        cost_estimate=cost(1, 1),
        name="middle",
    )(lists, got_first, got_second, table_vmem, sino)
    far, sino = lax.optimization_barrier((far, sino))
    sino, give = pl.pallas_call(
        functools.partial(main_kernel, slab=slab),
        out_shape=(sino_shape, shape((2 * piece, plane), jnp.float32)),
        in_specs=[vmem] * 6,
        out_specs=(vmem, vmem),
        scratch_shapes=index + window + rows_of(2 * piece) + picks_of(STATIC) + waits,
        compiler_params=room(16),
        cost_estimate=cost(1, 1),
        name="main",
    )(lists, far, table_vmem, turned, sino, decay)
    taken = send(give, swap)
    keep = pl.pallas_call(
        functools.partial(rest_kernel, group=0, slab=slab),
        out_shape=shape((2 * piece, plane), jnp.float32),
        in_specs=[vmem] * 4,
        out_specs=vmem,
        scratch_shapes=index + picks_of(STATIC) + waits,
        compiler_params=room(16),
        cost_estimate=cost(1, 1),
        name="rest",
    )(lists, turned, sino, decay)
    taken, keep = lax.optimization_barrier((taken, keep))
    wire = (keep + taken).astype(jnp.bfloat16)
    back_second = send(wire[piece:], back(second))
    back_first = send(wire[:piece], back(first))

    home = pl.pallas_call(
        functools.partial(rest_kernel, group=2, slab=slab),
        out_shape=shape((piece, plane), jnp.float32),
        in_specs=[vmem] * 4,
        out_specs=vmem,
        scratch_shapes=index + picks_of(8) + waits,
        compiler_params=room(16),
        cost_estimate=cost(1, 1),
        name="home",
    )(lists, turned, sino, decay)
    prior = pl.pallas_call(
        functools.partial(prior_kernel, devices=devices, here=here),
        out_shape=shape((part, plane), jnp.float32),
        in_specs=[vmem] * 5,
        out_specs=vmem,
        compiler_params=room(8),
        cost_estimate=cost(1, 1),
        name="prior",
    )(mine, other, got_first, got_second, far)
    back_second, back_first, home, prior = lax.optimization_barrier(
        (back_second, back_first, home, prior)
    )

    arrived = (back_second.astype(jnp.float32) + back_first.astype(jnp.float32)) + home
    passed = send(arrived[part:], swap)
    out = pl.pallas_call(
        last_kernel,
        out_shape=shape((part, strip, row), jnp.float32),
        in_specs=[vmem] * 3,
        out_specs=hbm,
        scratch_shapes=[
            pltpu.VMEM((part, strip, row), jnp.float32),
            pltpu.SemaphoreType.DMA((4,)),
        ],
        compiler_params=room(4),
        name="last",
    )(arrived[:part], passed, prior)
    return out.reshape(volume.shape)


def solution(mesh):
    in_specs = (
        P(AXES, None, None, None),
        P(AXES, None, None, None),
        P(AXES, None, None),
        P(AXES),
        P(AXES, None),
        P(AXES, None),
        P(AXES),
    )
    out_specs = P(AXES, None, None, None)
    return jax.shard_map(shards, mesh=mesh, in_specs=in_specs, out_specs=out_specs, check_vma=False)
```

profile of v0, /device:TPU:3, one launch (start us, length us, event | category | flops | bytes accessed | tf_op | source)
XLA Modules:
  0.0 29.1 jit_solution(3238802484106794372)
XLA Ops:
  0.0 0.7 %collective-permute-start = (f32[32,2,512]{2,1,0:T(2,128)}, f32[32,2,512]{2,1,0:T(2,128)S(1)}, u32[]{:S(2)}, u32[]{:S(2)}) collective-permute-start(f32[32,2,512]{2,1,0:T(2,128)} %bitcast.8), channel_id=1, source_target_pairs={{0,1},{1,0},{2,3},{3,2},{4,5},{5,4},{6,7},{7,6},{8,9},{9,8},{10,11... | collective-permute-start | bytes 393224 | tf_op jit(solution)/shard_map/ppermute | solution.py:497
  0.7 1.0 %load.1 = (f32[32,2,512]{2,1,0:T(2,128)S(1)}, bf16[32,1024]{1,0:T(8,128)(2,1)S(1)}) custom-call(f32[32,2,512]{2,1,0:T(2,128)} %bitcast.9), custom_call_target="tpu_custom_call" | custom-call | flops 1 | bytes 1 | tf_op jit(solution)/shard_map/load/pallas_call | solution.py:513
  1.7 0.1 collective-permute-done.other_ref
  1.9 0.2 join.1
  2.1 4.3 %collective-permute-start.2 = (bf16[528,128]{1,0:T(8,128)(2,1)S(1)}, bf16[528,128]{1,0:T(8,128)(2,1)S(1)}, u32[]{:S(2)}, u32[]{:S(2)}) collective-permute-start(bf16[528,128]{1,0:T(8,128)(2,1)S(1)} %get-tuple-element.40), channel_id=1, source_target_pairs={{2,6},{8,12},{10,14},{16,20},{18,22},{24,28},{3,5},{7,9},{11,13},{... | collective-permute-start | bytes 405512 | tf_op jit(solution)/shard_map/ppermute | solution.py:497
  6.4 0.0 collective-permute-start.1
  6.4 4.4 %early.1 = (bf16[1024,1792]{1,0:T(8,128)(2,1)S(1)}, bf16[1792,1024]{1,0:T(8,128)(2,1)S(1)}, s32[24,32]{1,0:T(8,128)S(1)}, f32[7,512,128]{2,1,0:T(8,128)S(1)}, f32[7,512,128]{2,1,0:T(8,128)S(1)}) custom-call(bf16[528,128]{1,0:T(8,128)(2,1)S(1)} %get-tuple-element.39.both_ref, bf16[2,1024,896]{2,1,0:T(8,128)(2,1)} %bitcast.7, ...), custom_call_target="tpu_custom_call" | custom-call | flops 1 | bytes 1 | tf_op jit(solution)/shard_map/early/pallas_call | solution.py:538
  10.7 0.1 collective-permute-done.2.first_ref
  10.9 0.7 %collective-permute-done.1.second_ref = bf16[528,128]{1,0:T(8,128)(2,1)S(1)} collective-permute-done((bf16[528,128]{1,0:T(8,128)(2,1)S(1)}, bf16[528,128]{1,0:T(8,128)(2,1)S(1)}, u32[]{:S(2)}, u32[]{:S(2)}) %collective-permute-start.1) | collective-permute-done | bytes 135200 | tf_op jit(solution)/shard_map/ppermute | solution.py:497
  11.6 0.9 %collective-permute-start.3 = (bf16[1056,128]{1,0:T(8,128)(2,1)S(1)}, bf16[1056,128]{1,0:T(8,128)(2,1)S(1)}, u32[]{:S(2)}, u32[]{:S(2)}) collective-permute-start(bf16[1056,128]{1,0:T(8,128)(2,1)S(1)} %pad_maximum_fusion), channel_id=1, source_target_pairs={{0,1},{1,0},{2,3},{3,2},{4,5},{5,4},{6,7},{7,6},{8,9},{9,8},{10,11... | collective-permute-start | bytes 811016 | tf_op jit(solution)/shard_map/ppermute | solution.py:497
  12.5 0.9 %middle.1.begun_ref = f32[7,512,128]{2,1,0:T(8,128)S(1)} custom-call(s32[24,32]{1,0:T(8,128)S(1)} %get-tuple-element.46.lists_ref, bf16[528,128]{1,0:T(8,128)(2,1)S(1)} %collective-permute-done.2.first_ref, bf16[528,128]{1,0:T(8,128)(2,1)S(1)} %collective-permute-done.1.second_ref, bf16[1024,1792]{1,0:T(8,128)(2,1)S(1)} %get-tuple-element.49.table_ref, ...), custom_call_target="tpu_custom_call" | custom-call | flops 1 | bytes 1 | tf_op jit(solution)/shard_map/middle/pallas_call | solution.py:597
  13.4 0.2 collective-permute-done.3.far_ref
  13.7 2.0 %main.1 = (f32[7,512,128]{2,1,0:T(8,128)S(1)}, f32[128,1024]{1,0:T(8,128)S(1)}) custom-call(s32[24,32]{1,0:T(8,128)S(1)} %get-tuple-element.46.lists_ref, bf16[1056,128]{1,0:T(8,128)(2,1)S(1)} %collective-permute-done.3.far_ref, bf16[1024,1792]{1,0:T(8,128)(2,1)S(1)} %get-tuple-element.49.table_ref, bf16[1792,1024]{1,0:T(8,128)(2,1)S(1)} %get-tuple-element.52.turned_ref, ...), custom_call_target="tpu_custom_call" | custom-call | flops 1 | bytes 1 | tf_op jit(solution)/shard_map/main/pallas_call | solution.py:608
  15.6 0.6 %collective-permute-start.4 = (f32[128,1024]{1,0:T(8,128)S(1)}, f32[128,1024]{1,0:T(8,128)S(1)}, u32[]{:S(2)}, u32[]{:S(2)}) collective-permute-start(f32[128,1024]{1,0:T(8,128)S(1)} %get-tuple-element.55), channel_id=1, source_target_pairs={{0,1},{1,0},{2,3},{3,2},{4,5},{5,4},{6,7},{7,6},{8,9},{9,8},{10,11... | collective-permute-start | bytes 1572872 | tf_op jit(solution)/shard_map/ppermute | solution.py:497
  16.3 1.9 %rest.1 = f32[128,1024]{1,0:T(8,128)S(1)} custom-call(s32[24,32]{1,0:T(8,128)S(1)} %get-tuple-element.46.lists_ref, bf16[1792,1024]{1,0:T(8,128)(2,1)S(1)} %get-tuple-element.52.turned_ref, f32[7,512,128]{2,1,0:T(8,128)S(1)} %get-tuple-element.56.sino_ref, f32[7,512,128]{2,1,0:T(8,128)S(1)} %get-tuple-element.54.decay_ref), custom_call_target="tpu_custom_call" | custom-call | flops 1 | bytes 1 | tf_op jit(solution)/shard_map/rest/pallas_call | solution.py:619
  18.2 0.0 collective-permute-done.4
  18.2 0.1 add_convert_fusion
  18.3 2.8 %collective-permute-start.6 = (bf16[64,1024]{1,0:T(8,128)(2,1)S(1)}, bf16[64,1024]{1,0:T(8,128)(2,1)S(1)}, u32[]{:S(2)}, u32[]{:S(2)}) collective-permute-start(bf16[64,1024]{1,0:T(8,128)(2,1)S(1)} %get-tuple-element.65), channel_id=1, source_target_pairs={{6,2},{12,8},{14,10},{20,16},{22,18},{28,24},{5,3},{9,7},{13,11},{... | collective-permute-start | bytes 393224 | tf_op jit(solution)/shard_map/ppermute | solution.py:497
  21.0 0.0 collective-permute-start.5
  21.0 0.2 prior.1.prior_ref
  21.2 1.5 %home.1 = f32[64,1024]{1,0:T(8,128)S(1)} custom-call(s32[24,32]{1,0:T(8,128)S(1)} %get-tuple-element.46.lists_ref, bf16[1792,1024]{1,0:T(8,128)(2,1)S(1)} %get-tuple-element.52.turned_ref, f32[7,512,128]{2,1,0:T(8,128)S(1)} %get-tuple-element.56.sino_ref, f32[7,512,128]{2,1,0:T(8,128)S(1)} %get-tuple-element.54.decay_ref), custom_call_target="tpu_custom_call" | custom-call | flops 1 | bytes 1 | tf_op jit(solution)/shard_map/home/pallas_call | solution.py:634
  22.7 4.2 %collective-permute-done.6 = bf16[64,1024]{1,0:T(8,128)(2,1)S(1)} collective-permute-done((bf16[64,1024]{1,0:T(8,128)(2,1)S(1)}, bf16[64,1024]{1,0:T(8,128)(2,1)S(1)}, u32[]{:S(2)}, u32[]{:S(2)}) %collective-permute-start.6) | collective-permute-done | bytes 131104 | tf_op jit(solution)/shard_map/ppermute | solution.py:497
  26.9 0.0 collective-permute-done.5
  27.0 0.1 collective-permute-start.7
  27.1 1.3 %collective-permute-done.7.passed_ref = f32[32,1024]{1,0:T(8,128)S(1)} collective-permute-done((f32[32,1024]{1,0:T(8,128)S(1)}, f32[32,1024]{1,0:T(8,128)S(1)}, u32[]{:S(2)}, u32[]{:S(2)}) %collective-permute-start.7) | collective-permute-done | bytes 131104 | tf_op jit(solution)/shard_map/ppermute | solution.py:497
  28.4 0.7 %last.1 = f32[32,2,512]{2,1,0:T(2,128)} custom-call(f32[32,1024]{1,0:T(8,128)S(1)} %get-tuple-element.64.arrived_ref, f32[32,1024]{1,0:T(8,128)S(1)} %collective-permute-done.7.passed_ref, f32[32,1024]{1,0:T(8,128)S(1)} %prior.1.prior_ref), custom_call_target="tpu_custom_call" | custom-call | tf_op jit(solution)/shard_map/last/pallas_call | solution.py:659
  (4 shorter events, 0.1 us)
Async XLA Ops:
  0.0 1.9 %collective-permute-start = (f32[32,2,512]{2,1,0:T(2,128)}, f32[32,2,512]{2,1,0:T(2,128)S(1)}, u32[]{:S(2)}, u32[]{:S(2)}) collective-permute-start(f32[32,2,512]{2,1,0:T(2,128)} %bitcast.8), channel_id=1, source_target_pairs={{0,1},{1,0},{2,3},{3,2},{4,5},{5,4},{6,7},{7,6},{8,9},{9,8},{10,11... | collective-permute-start | bytes 393224 | tf_op jit(solution)/shard_map/ppermute | solution.py:497
  2.1 8.8 %collective-permute-start.2 = (bf16[528,128]{1,0:T(8,128)(2,1)S(1)}, bf16[528,128]{1,0:T(8,128)(2,1)S(1)}, u32[]{:S(2)}, u32[]{:S(2)}) collective-permute-start(bf16[528,128]{1,0:T(8,128)(2,1)S(1)} %get-tuple-element.40), channel_id=1, source_target_pairs={{2,6},{8,12},{10,14},{16,20},{18,22},{24,28},{3,5},{7,9},{11,13},{... | collective-permute-start | bytes 405512 | tf_op jit(solution)/shard_map/ppermute | solution.py:497
  6.4 5.2 %collective-permute-start.1 = (bf16[528,128]{1,0:T(8,128)(2,1)S(1)}, bf16[528,128]{1,0:T(8,128)(2,1)S(1)}, u32[]{:S(2)}, u32[]{:S(2)}) collective-permute-start(bf16[528,128]{1,0:T(8,128)(2,1)S(1)} %get-tuple-element.39.both_ref), channel_id=1, source_target_pairs={{4,8},{6,10},{12,16},{14,18},{20,24},{22,26},{0,2},{28,30},{1,3},{... | collective-permute-start | bytes 405512 | tf_op jit(solution)/shard_map/ppermute | solution.py:497
  11.6 2.1 %collective-permute-start.3 = (bf16[1056,128]{1,0:T(8,128)(2,1)S(1)}, bf16[1056,128]{1,0:T(8,128)(2,1)S(1)}, u32[]{:S(2)}, u32[]{:S(2)}) collective-permute-start(bf16[1056,128]{1,0:T(8,128)(2,1)S(1)} %pad_maximum_fusion), channel_id=1, source_target_pairs={{0,1},{1,0},{2,3},{3,2},{4,5},{5,4},{6,7},{7,6},{8,9},{9,8},{10,11... | collective-permute-start | bytes 811016 | tf_op jit(solution)/shard_map/ppermute | solution.py:497
  15.6 2.5 %collective-permute-start.4 = (f32[128,1024]{1,0:T(8,128)S(1)}, f32[128,1024]{1,0:T(8,128)S(1)}, u32[]{:S(2)}, u32[]{:S(2)}) collective-permute-start(f32[128,1024]{1,0:T(8,128)S(1)} %get-tuple-element.55), channel_id=1, source_target_pairs={{0,1},{1,0},{2,3},{3,2},{4,5},{5,4},{6,7},{7,6},{8,9},{9,8},{10,11... | collective-permute-start | bytes 1572872 | tf_op jit(solution)/shard_map/ppermute | solution.py:497
  18.3 8.7 %collective-permute-start.6 = (bf16[64,1024]{1,0:T(8,128)(2,1)S(1)}, bf16[64,1024]{1,0:T(8,128)(2,1)S(1)}, u32[]{:S(2)}, u32[]{:S(2)}) collective-permute-start(bf16[64,1024]{1,0:T(8,128)(2,1)S(1)} %get-tuple-element.65), channel_id=1, source_target_pairs={{6,2},{12,8},{14,10},{20,16},{22,18},{28,24},{5,3},{9,7},{13,11},{... | collective-permute-start | bytes 393224 | tf_op jit(solution)/shard_map/ppermute | solution.py:497
  21.0 5.9 %collective-permute-start.5 = (bf16[64,1024]{1,0:T(8,128)(2,1)S(1)}, bf16[64,1024]{1,0:T(8,128)(2,1)S(1)}, u32[]{:S(2)}, u32[]{:S(2)}) collective-permute-start(bf16[64,1024]{1,0:T(8,128)(2,1)S(1)} %get-tuple-element.66), channel_id=1, source_target_pairs={{8,4},{10,6},{16,12},{18,14},{24,20},{26,22},{2,0},{30,28},{3,1},{... | collective-permute-start | bytes 393224 | tf_op jit(solution)/shard_map/ppermute | solution.py:497
  27.0 1.4 %collective-permute-start.7 = (f32[32,1024]{1,0:T(8,128)S(1)}, f32[32,1024]{1,0:T(8,128)S(1)}, u32[]{:S(2)}, u32[]{:S(2)}) collective-permute-start(f32[32,1024]{1,0:T(8,128)S(1)} %get-tuple-element.63), channel_id=1, source_target_pairs={{0,1},{1,0},{2,3},{3,2},{4,5},{5,4},{6,7},{7,6},{8,9},{9,8},{10,11... | collective-permute-start | bytes 393224 | tf_op jit(solution)/shard_map/ppermute | solution.py:497
where the time goes:
time: 29.1 us
  Pallas kernels  12.8 us (44%)
  starting transfers between devices  9.32 us (32%)
  waiting for transfers between devices  6.78 us (23%)
    ppermute x8, starting transfers between devices, shards(): send = lambda value, pairs: lax.ppermute(value, AXES, pairs)  9.32 us
    ppermute x8, waiting for transfers between devices, shards(): send = lambda value, pairs: lax.ppermute(value, AXES, pairs)  6.78 us
    pallas_call x1, Pallas kernels, shards(): pl.pallas_call(functools.partial(early_kernel, piece=piece, chips=devices...  4.36 us
    pallas_call x1, Pallas kernels, shards(): pl.pallas_call(functools.partial(main_kernel, slab=slab), out_shape=(sino...  1.99 us
    pallas_call x1, Pallas kernels, shards(): pl.pallas_call(functools.partial(rest_kernel, group=0, slab=slab), out_sh...  1.89 us
    pallas_call x1, Pallas kernels, shards(): pl.pallas_call(functools.partial(rest_kernel, group=2, slab=slab), out_sh...  1.46 us
    pallas_call x1, Pallas kernels, shards(): pl.pallas_call(load_kernel, out_shape=(shape(flat.shape, flat.dtype), sha...  1.04 us
    pallas_call x1, Pallas kernels, shards(): pl.pallas_call(functools.partial(middle_kernel, slab=slab), out_shape=sin...  0.93 us
  transfers between devices with their start and end apart: 8, of which 6 were waited for; matrix products, arithmetic and copies ran while one was open for 0% of the time, Pallas kernels for 34%

commit v1 on v0

--- a/solution.py
+++ b/solution.py
@@ -8,7 +8,8 @@
 from jax.sharding import PartitionSpec as P
 
 AXES = ("grp", "view")
-STATIC = 12
+STATIC = 16
+LEVELS = (8, 10, 12)
 MORE = 4
 DELTA = 0.5
 PRIOR_WEIGHT = 2.0
@@ -241,9 +242,17 @@
 
         return add
 
-    spread[...] = jnp.dot(
-        picked[0:static_rows, :], turned_ref[...], preferred_element_type=jnp.float32
-    )
+    least = -1
+    for most in [m for m in LEVELS if m < static] + [static]:
+        rows = most * slab
+
+        @pl.when((blocks > least) & ((blocks <= most) | (most == static)))
+        def _():
+            spread[0:rows, :] = jnp.dot(
+                picked[0:rows, :], turned_ref[...], preferred_element_type=jnp.float32
+            )
+
+        least = most
     lax.fori_loop(0, jnp.minimum(blocks, static), add_from(0), 0)
 
     def further(c, carry):
@@ -627,9 +636,9 @@
         name="rest",
     )(lists, turned, sino, decay)
     taken, keep = lax.optimization_barrier((taken, keep))
-    wire = (keep + taken).astype(jnp.bfloat16)
-    back_second = send(wire[piece:], back(second))
-    back_first = send(wire[:piece], back(first))
+    wire = lambda rows: (keep[rows] + taken[rows]).astype(jnp.bfloat16)
+    back_second = send(wire(slice(piece, 2 * piece)), back(second))
+    back_first = send(wire(slice(0, piece)), back(first))
 
     home = pl.pallas_call(
         functools.partial(rest_kernel, group=2, slab=slab),
@@ -654,8 +663,10 @@
         (back_second, back_first, home, prior)
     )
 
-    arrived = (back_second.astype(jnp.float32) + back_first.astype(jnp.float32)) + home
-    passed = send(arrived[part:], swap)
+    arrived = lambda rows: (
+        back_second[rows].astype(jnp.float32) + back_first[rows].astype(jnp.float32)
+    ) + home[rows]
+    passed = send(arrived(slice(part, piece)), swap)
     out = pl.pallas_call(
         last_kernel,
         out_shape=shape((part, strip, row), jnp.float32),
@@ -667,7 +678,7 @@
         ],
         compiler_params=room(4),
         name="last",
-    )(arrived[:part], passed, prior)
+    )(arrived(slice(0, part)), passed, prior)
     return out.reshape(volume.shape)
 
 

time: 29.1 us -> 28.5 us (0.979)
  Pallas kernels: 12.8 us -> 12 us
  waiting for transfers between devices: 6.78 us -> 6.09 us
  starting transfers between devices: 9.32 us -> 9.99 us
    ppermute x8, waiting for transfers between devices: 6.78 us -> 6.09 us  [shards(): send = lambda value, pairs: lax.ppermute(value, AXES, pairs)]
    ppermute x8, starting transfers between devices: 9.32 us -> 9.99 us  [shards(): send = lambda value, pairs: lax.ppermute(value, AXES, pairs)]
    pallas_call x1, Pallas kernels: 1.89 us -> 1.5 us  [shards(): pl.pallas_call(functools.partial(rest_kernel, group=0, slab=slab), out_sh...]
  transfers between devices with their start and end apart: 8 -> 8, of which waited for: 6 -> 8; matrix products, arithmetic and copies ran while one was open for 0% -> 0% of each run, Pallas kernels for 34% -> 33%
where the time goes in v1:
time: 28.5 us; the launch traced here: 28.3 us
  Pallas kernels  12 us (42%)
  starting transfers between devices  9.99 us (35%)
  waiting for transfers between devices  6.09 us (21%)
    ppermute x8, starting transfers between devices, shards(): send = lambda value, pairs: lax.ppermute(value, AXES, pairs)  9.99 us
    ppermute x8, waiting for transfers between devices, shards(): send = lambda value, pairs: lax.ppermute(value, AXES, pairs)  6.09 us
    pallas_call x1, Pallas kernels, shards(): pl.pallas_call(functools.partial(early_kernel, piece=piece, chips=devices...  4.34 us
    pallas_call x1, Pallas kernels, shards(): pl.pallas_call(functools.partial(main_kernel, slab=slab), out_shape=(sino...  1.8 us
    pallas_call x1, Pallas kernels, shards(): pl.pallas_call(functools.partial(rest_kernel, group=0, slab=slab), out_sh...  1.5 us
    pallas_call x1, Pallas kernels, shards(): pl.pallas_call(functools.partial(rest_kernel, group=2, slab=slab), out_sh...  1.45 us
    pallas_call x1, Pallas kernels, shards(): pl.pallas_call(load_kernel, out_shape=(shape(flat.shape, flat.dtype), sha...  1.04 us
    pallas_call x1, Pallas kernels, shards(): pl.pallas_call(functools.partial(middle_kernel, slab=slab), out_shape=sin...  0.82 us
  transfers between devices with their start and end apart: 8, of which 8 were waited for; matrix products, arithmetic and copies ran while one was open for 0% of the time, Pallas kernels for 33%

profile of v1, /device:TPU:3, one launch (start us, length us, event | category | flops | bytes accessed | tf_op | source)
XLA Modules:
  0.0 28.3 jit_solution(17607704409249362516)
XLA Ops:
  0.0 0.7 %collective-permute-start = (f32[32,2,512]{2,1,0:T(2,128)}, f32[32,2,512]{2,1,0:T(2,128)S(1)}, u32[]{:S(2)}, u32[]{:S(2)}) collective-permute-start(f32[32,2,512]{2,1,0:T(2,128)} %bitcast.8), channel_id=1, source_target_pairs={{0,1},{1,0},{2,3},{3,2},{4,5},{5,4},{6,7},{7,6},{8,9},{9,8},{10,11... | collective-permute-start | bytes 393224 | tf_op jit(solution)/shard_map/ppermute | solution.py:506
  0.7 1.0 %load.1 = (f32[32,2,512]{2,1,0:T(2,128)S(1)}, bf16[32,1024]{1,0:T(8,128)(2,1)S(1)}) custom-call(f32[32,2,512]{2,1,0:T(2,128)} %bitcast.9), custom_call_target="tpu_custom_call" | custom-call | flops 1 | bytes 1 | tf_op jit(solution)/shard_map/load/pallas_call | solution.py:522
  1.7 0.1 collective-permute-done.other_ref
  1.9 0.2 join.1
  2.1 4.3 %collective-permute-start.2 = (bf16[528,128]{1,0:T(8,128)(2,1)S(1)}, bf16[528,128]{1,0:T(8,128)(2,1)S(1)}, u32[]{:S(2)}, u32[]{:S(2)}) collective-permute-start(bf16[528,128]{1,0:T(8,128)(2,1)S(1)} %get-tuple-element.40), channel_id=1, source_target_pairs={{2,6},{8,12},{10,14},{16,20},{18,22},{24,28},{3,5},{7,9},{11,13},{... | collective-permute-start | bytes 405512 | tf_op jit(solution)/shard_map/ppermute | solution.py:506
  6.4 0.0 collective-permute-start.1
  6.4 4.3 %early.1 = (bf16[1024,1792]{1,0:T(8,128)(2,1)S(1)}, bf16[1792,1024]{1,0:T(8,128)(2,1)S(1)}, s32[24,32]{1,0:T(8,128)S(1)}, f32[7,512,128]{2,1,0:T(8,128)S(1)}, f32[7,512,128]{2,1,0:T(8,128)S(1)}) custom-call(bf16[528,128]{1,0:T(8,128)(2,1)S(1)} %get-tuple-element.39.both_ref, bf16[2,1024,896]{2,1,0:T(8,128)(2,1)} %bitcast.7, ...), custom_call_target="tpu_custom_call" | custom-call | flops 1 | bytes 1 | tf_op jit(solution)/shard_map/early/pallas_call | solution.py:547
  10.7 0.1 collective-permute-done.2.first_ref
  10.9 0.7 %collective-permute-done.1.second_ref = bf16[528,128]{1,0:T(8,128)(2,1)S(1)} collective-permute-done((bf16[528,128]{1,0:T(8,128)(2,1)S(1)}, bf16[528,128]{1,0:T(8,128)(2,1)S(1)}, u32[]{:S(2)}, u32[]{:S(2)}) %collective-permute-start.1) | collective-permute-done | bytes 135200 | tf_op jit(solution)/shard_map/ppermute | solution.py:506
  11.6 0.9 %collective-permute-start.3 = (bf16[1056,128]{1,0:T(8,128)(2,1)S(1)}, bf16[1056,128]{1,0:T(8,128)(2,1)S(1)}, u32[]{:S(2)}, u32[]{:S(2)}) collective-permute-start(bf16[1056,128]{1,0:T(8,128)(2,1)S(1)} %pad_maximum_fusion), channel_id=1, source_target_pairs={{0,1},{1,0},{2,3},{3,2},{4,5},{5,4},{6,7},{7,6},{8,9},{9,8},{10,11... | collective-permute-start | bytes 811016 | tf_op jit(solution)/shard_map/ppermute | solution.py:506
  12.5 0.8 %middle.1.begun_ref = f32[7,512,128]{2,1,0:T(8,128)S(1)} custom-call(s32[24,32]{1,0:T(8,128)S(1)} %get-tuple-element.46.lists_ref, bf16[528,128]{1,0:T(8,128)(2,1)S(1)} %collective-permute-done.2.first_ref, bf16[528,128]{1,0:T(8,128)(2,1)S(1)} %collective-permute-done.1.second_ref, bf16[1024,1792]{1,0:T(8,128)(2,1)S(1)} %get-tuple-element.49.table_ref, ...), custom_call_target="tpu_custom_call" | custom-call | flops 1 | bytes 1 | tf_op jit(solution)/shard_map/middle/pallas_call | solution.py:606
  13.3 0.3 %collective-permute-done.3.far_ref = bf16[1056,128]{1,0:T(8,128)(2,1)S(1)} collective-permute-done((bf16[1056,128]{1,0:T(8,128)(2,1)S(1)}, bf16[1056,128]{1,0:T(8,128)(2,1)S(1)}, u32[]{:S(2)}, u32[]{:S(2)}) %collective-permute-start.3) | collective-permute-done | bytes 270368 | tf_op jit(solution)/shard_map/ppermute | solution.py:506
  13.7 1.8 %main.1 = (f32[7,512,128]{2,1,0:T(8,128)S(1)}, f32[128,1024]{1,0:T(8,128)S(1)}) custom-call(s32[24,32]{1,0:T(8,128)S(1)} %get-tuple-element.46.lists_ref, bf16[1056,128]{1,0:T(8,128)(2,1)S(1)} %collective-permute-done.3.far_ref, bf16[1024,1792]{1,0:T(8,128)(2,1)S(1)} %get-tuple-element.49.table_ref, bf16[1792,1024]{1,0:T(8,128)(2,1)S(1)} %get-tuple-element.52.turned_ref, ...), custom_call_target="tpu_custom_call" | custom-call | flops 1 | bytes 1 | tf_op jit(solution)/shard_map/main/pallas_call | solution.py:617
  15.5 0.3 %collective-permute-start.4 = (f32[128,1024]{1,0:T(8,128)S(1)}, f32[128,1024]{1,0:T(8,128)S(1)}, u32[]{:S(2)}, u32[]{:S(2)}) collective-permute-start(f32[128,1024]{1,0:T(8,128)S(1)} %get-tuple-element.55), channel_id=1, source_target_pairs={{0,1},{1,0},{2,3},{3,2},{4,5},{5,4},{6,7},{7,6},{8,9},{9,8},{10,11... | collective-permute-start | bytes 1572872 | tf_op jit(solution)/shard_map/ppermute | solution.py:506
  15.8 1.5 %rest.1 = f32[128,1024]{1,0:T(8,128)S(1)} custom-call(s32[24,32]{1,0:T(8,128)S(1)} %get-tuple-element.46.lists_ref, bf16[1792,1024]{1,0:T(8,128)(2,1)S(1)} %get-tuple-element.52.turned_ref, f32[7,512,128]{2,1,0:T(8,128)S(1)} %get-tuple-element.56.sino_ref, f32[7,512,128]{2,1,0:T(8,128)S(1)} %get-tuple-element.54.decay_ref), custom_call_target="tpu_custom_call" | custom-call | flops 1 | bytes 1 | tf_op jit(solution)/shard_map/rest/pallas_call | solution.py:628
  17.3 0.1 collective-permute-done.4
  17.4 0.1 add_convert_fusion
  17.5 3.5 %collective-permute-start.6 = (bf16[64,1024]{1,0:T(8,128)(2,1)S(1)}, bf16[64,1024]{1,0:T(8,128)(2,1)S(1)}, u32[]{:S(2)}, u32[]{:S(2)}) collective-permute-start(bf16[64,1024]{1,0:T(8,128)(2,1)S(1)} %get-tuple-element.63), channel_id=1, source_target_pairs={{6,2},{12,8},{14,10},{20,16},{22,18},{28,24},{5,3},{9,7},{13,11},{... | collective-permute-start | bytes 393224 | tf_op jit(solution)/shard_map/ppermute | solution.py:506
  20.9 0.0 collective-permute-start.5
  20.9 0.2 prior.1.prior_ref
  21.2 1.5 %home.1 = f32[64,1024]{1,0:T(8,128)S(1)} custom-call(s32[24,32]{1,0:T(8,128)S(1)} %get-tuple-element.46.lists_ref, bf16[1792,1024]{1,0:T(8,128)(2,1)S(1)} %get-tuple-element.52.turned_ref, f32[7,512,128]{2,1,0:T(8,128)S(1)} %get-tuple-element.56.sino_ref, f32[7,512,128]{2,1,0:T(8,128)S(1)} %get-tuple-element.54.decay_ref), custom_call_target="tpu_custom_call" | custom-call | flops 1 | bytes 1 | tf_op jit(solution)/shard_map/home/pallas_call | solution.py:643
  22.6 3.2 %collective-permute-done.6 = bf16[64,1024]{1,0:T(8,128)(2,1)S(1)} collective-permute-done((bf16[64,1024]{1,0:T(8,128)(2,1)S(1)}, bf16[64,1024]{1,0:T(8,128)(2,1)S(1)}, u32[]{:S(2)}, u32[]{:S(2)}) %collective-permute-start.6) | collective-permute-done | bytes 131104 | tf_op jit(solution)/shard_map/ppermute | solution.py:506
  25.8 0.4 %collective-permute-done.5 = bf16[64,1024]{1,0:T(8,128)(2,1)S(1)} collective-permute-done((bf16[64,1024]{1,0:T(8,128)(2,1)S(1)}, bf16[64,1024]{1,0:T(8,128)(2,1)S(1)}, u32[]{:S(2)}, u32[]{:S(2)}) %collective-permute-start.5) | collective-permute-done | bytes 131104 | tf_op jit(solution)/shard_map/ppermute | solution.py:506
  26.2 0.3 %collective-permute-start.7 = (f32[32,1024]{1,0:T(8,128)S(1)}, f32[32,1024]{1,0:T(8,128)S(1)}, u32[]{:S(2)}, u32[]{:S(2)}) collective-permute-start(f32[32,1024]{1,0:T(8,128)S(1)} %get-tuple-element.65), channel_id=1, source_target_pairs={{0,1},{1,0},{2,3},{3,2},{4,5},{5,4},{6,7},{7,6},{8,9},{9,8},{10,11... | collective-permute-start | bytes 393224 | tf_op jit(solution)/shard_map/ppermute | solution.py:506
  26.5 1.1 %collective-permute-done.7.passed_ref = f32[32,1024]{1,0:T(8,128)S(1)} collective-permute-done((f32[32,1024]{1,0:T(8,128)S(1)}, f32[32,1024]{1,0:T(8,128)S(1)}, u32[]{:S(2)}, u32[]{:S(2)}) %collective-permute-start.7) | collective-permute-done | bytes 131104 | tf_op jit(solution)/shard_map/ppermute | solution.py:506
  27.6 0.7 %last.1 = f32[32,2,512]{2,1,0:T(2,128)} custom-call(f32[32,1024]{1,0:T(8,128)S(1)} %get-tuple-element.66.arrived_ref, f32[32,1024]{1,0:T(8,128)S(1)} %collective-permute-done.7.passed_ref, f32[32,1024]{1,0:T(8,128)S(1)} %prior.1.prior_ref), custom_call_target="tpu_custom_call" | custom-call | tf_op jit(solution)/shard_map/last/pallas_call | solution.py:670
  (2 shorter events, 0.1 us)
Async XLA Ops:
  0.0 1.9 %collective-permute-start = (f32[32,2,512]{2,1,0:T(2,128)}, f32[32,2,512]{2,1,0:T(2,128)S(1)}, u32[]{:S(2)}, u32[]{:S(2)}) collective-permute-start(f32[32,2,512]{2,1,0:T(2,128)} %bitcast.8), channel_id=1, source_target_pairs={{0,1},{1,0},{2,3},{3,2},{4,5},{5,4},{6,7},{7,6},{8,9},{9,8},{10,11... | collective-permute-start | bytes 393224 | tf_op jit(solution)/shard_map/ppermute | solution.py:506
  2.1 8.8 %collective-permute-start.2 = (bf16[528,128]{1,0:T(8,128)(2,1)S(1)}, bf16[528,128]{1,0:T(8,128)(2,1)S(1)}, u32[]{:S(2)}, u32[]{:S(2)}) collective-permute-start(bf16[528,128]{1,0:T(8,128)(2,1)S(1)} %get-tuple-element.40), channel_id=1, source_target_pairs={{2,6},{8,12},{10,14},{16,20},{18,22},{24,28},{3,5},{7,9},{11,13},{... | collective-permute-start | bytes 405512 | tf_op jit(solution)/shard_map/ppermute | solution.py:506
  6.4 5.2 %collective-permute-start.1 = (bf16[528,128]{1,0:T(8,128)(2,1)S(1)}, bf16[528,128]{1,0:T(8,128)(2,1)S(1)}, u32[]{:S(2)}, u32[]{:S(2)}) collective-permute-start(bf16[528,128]{1,0:T(8,128)(2,1)S(1)} %get-tuple-element.39.both_ref), channel_id=1, source_target_pairs={{4,8},{6,10},{12,16},{14,18},{20,24},{22,26},{0,2},{28,30},{1,3},{... | collective-permute-start | bytes 405512 | tf_op jit(solution)/shard_map/ppermute | solution.py:506
  11.6 2.1 %collective-permute-start.3 = (bf16[1056,128]{1,0:T(8,128)(2,1)S(1)}, bf16[1056,128]{1,0:T(8,128)(2,1)S(1)}, u32[]{:S(2)}, u32[]{:S(2)}) collective-permute-start(bf16[1056,128]{1,0:T(8,128)(2,1)S(1)} %pad_maximum_fusion), channel_id=1, source_target_pairs={{0,1},{1,0},{2,3},{3,2},{4,5},{5,4},{6,7},{7,6},{8,9},{9,8},{10,11... | collective-permute-start | bytes 811016 | tf_op jit(solution)/shard_map/ppermute | solution.py:506
  15.5 2.0 %collective-permute-start.4 = (f32[128,1024]{1,0:T(8,128)S(1)}, f32[128,1024]{1,0:T(8,128)S(1)}, u32[]{:S(2)}, u32[]{:S(2)}) collective-permute-start(f32[128,1024]{1,0:T(8,128)S(1)} %get-tuple-element.55), channel_id=1, source_target_pairs={{0,1},{1,0},{2,3},{3,2},{4,5},{5,4},{6,7},{7,6},{8,9},{9,8},{10,11... | collective-permute-start | bytes 1572872 | tf_op jit(solution)/shard_map/ppermute | solution.py:506
  17.5 8.3 %collective-permute-start.6 = (bf16[64,1024]{1,0:T(8,128)(2,1)S(1)}, bf16[64,1024]{1,0:T(8,128)(2,1)S(1)}, u32[]{:S(2)}, u32[]{:S(2)}) collective-permute-start(bf16[64,1024]{1,0:T(8,128)(2,1)S(1)} %get-tuple-element.63), channel_id=1, source_target_pairs={{6,2},{12,8},{14,10},{20,16},{22,18},{28,24},{5,3},{9,7},{13,11},{... | collective-permute-start | bytes 393224 | tf_op jit(solution)/shard_map/ppermute | solution.py:506
  20.9 5.2 %collective-permute-start.5 = (bf16[64,1024]{1,0:T(8,128)(2,1)S(1)}, bf16[64,1024]{1,0:T(8,128)(2,1)S(1)}, u32[]{:S(2)}, u32[]{:S(2)}) collective-permute-start(bf16[64,1024]{1,0:T(8,128)(2,1)S(1)} %get-tuple-element.64), channel_id=1, source_target_pairs={{8,4},{10,6},{16,12},{18,14},{24,20},{26,22},{2,0},{30,28},{3,1},{... | collective-permute-start | bytes 393224 | tf_op jit(solution)/shard_map/ppermute | solution.py:506
  26.2 1.4 %collective-permute-start.7 = (f32[32,1024]{1,0:T(8,128)S(1)}, f32[32,1024]{1,0:T(8,128)S(1)}, u32[]{:S(2)}, u32[]{:S(2)}) collective-permute-start(f32[32,1024]{1,0:T(8,128)S(1)} %get-tuple-element.65), channel_id=1, source_target_pairs={{0,1},{1,0},{2,3},{3,2},{4,5},{5,4},{6,7},{7,6},{8,9},{9,8},{10,11... | collective-permute-start | bytes 393224 | tf_op jit(solution)/shard_map/ppermute | solution.py:506

commit v2 on v1

--- a/solution.py
+++ b/solution.py
@@ -334,11 +334,11 @@
     load.wait()
     list_pairs(scal, lists, seen, height, held, 2 * piece, det_rows, tables, slab)
     save = fetch(lists, lists_ref, sems.at[0])
-    for table in range(tables):
-        copies[5 + table].wait()
-        cols = slice(table * channels, (table + 1) * channels)
-        turned_ref[cols, :] = table_ref[:, cols].T
+    for copy in copies[5:]:
+        copy.wait()
     proj[...] = jnp.dot(window[...], table_ref[...], preferred_element_type=jnp.float32)
+    for at in range(0, tables * channels, 128):
+        turned_ref[at : at + 128, :] = table_ref[:, at : at + 128].T
     place(Pairs(lists, 2 * Pairs.ROWS), sino_ref, proj, slab)
     save.wait()
 

time: 28.5 us -> 28.5 us (level)
  starting transfers between devices: 9.99 us -> 9.33 us
  waiting for transfers between devices: 6.09 us -> 6.62 us
    ppermute x8, starting transfers between devices: 9.99 us -> 9.33 us  [shards(): send = lambda value, pairs: lax.ppermute(value, AXES, pairs)]
    ppermute x8, waiting for transfers between devices: 6.09 us -> 6.62 us  [shards(): send = lambda value, pairs: lax.ppermute(value, AXES, pairs)]
    pallas_call x1, Pallas kernels: 1.8 us -> 2.13 us  [shards(): pl.pallas_call(functools.partial(main_kernel, slab=slab), out_shape=(sino...]
  transfers between devices with their start and end apart: 8 -> 8, of which waited for: 8 -> 7; matrix products, arithmetic and copies ran while one was open for 0% -> 0% of each run, Pallas kernels for 33% -> 32%
where the time goes in v2:
time: 28.5 us; the launch traced here: 28.2 us
  Pallas kernels  12.1 us (42%)
  starting transfers between devices  9.33 us (33%)
  waiting for transfers between devices  6.62 us (23%)
    ppermute x8, starting transfers between devices, shards(): send = lambda value, pairs: lax.ppermute(value, AXES, pairs)  9.33 us
    ppermute x8, waiting for transfers between devices, shards(): send = lambda value, pairs: lax.ppermute(value, AXES, pairs)  6.62 us
    pallas_call x1, Pallas kernels, shards(): pl.pallas_call(functools.partial(early_kernel, piece=piece, chips=devices...  4.12 us
    pallas_call x1, Pallas kernels, shards(): pl.pallas_call(functools.partial(main_kernel, slab=slab), out_shape=(sino...  2.13 us
    pallas_call x1, Pallas kernels, shards(): pl.pallas_call(functools.partial(rest_kernel, group=0, slab=slab), out_sh...  1.49 us
    pallas_call x1, Pallas kernels, shards(): pl.pallas_call(functools.partial(rest_kernel, group=2, slab=slab), out_sh...  1.4 us
    pallas_call x1, Pallas kernels, shards(): pl.pallas_call(load_kernel, out_shape=(shape(flat.shape, flat.dtype), sha...  1.04 us
    pallas_call x1, Pallas kernels, shards(): pl.pallas_call(functools.partial(middle_kernel, slab=slab), out_shape=sin...  0.8 us
  transfers between devices with their start and end apart: 8, of which 7 were waited for; matrix products, arithmetic and copies ran while one was open for 0% of the time, Pallas kernels for 32%

profile of v2, /device:TPU:3, one launch (start us, length us, event | category | flops | bytes accessed | tf_op | source)
XLA Modules:
  0.0 28.2 jit_solution(6754053855226426302)
XLA Ops:
  0.0 0.7 %collective-permute-start = (f32[32,2,512]{2,1,0:T(2,128)}, f32[32,2,512]{2,1,0:T(2,128)S(1)}, u32[]{:S(2)}, u32[]{:S(2)}) collective-permute-start(f32[32,2,512]{2,1,0:T(2,128)} %bitcast.8), channel_id=1, source_target_pairs={{0,1},{1,0},{2,3},{3,2},{4,5},{5,4},{6,7},{7,6},{8,9},{9,8},{10,11... | collective-permute-start | bytes 393224 | tf_op jit(solution)/shard_map/ppermute | solution.py:506
  0.7 1.0 %load.1 = (f32[32,2,512]{2,1,0:T(2,128)S(1)}, bf16[32,1024]{1,0:T(8,128)(2,1)S(1)}) custom-call(f32[32,2,512]{2,1,0:T(2,128)} %bitcast.9), custom_call_target="tpu_custom_call" | custom-call | flops 1 | bytes 1 | tf_op jit(solution)/shard_map/load/pallas_call | solution.py:522
  1.7 0.1 collective-permute-done.other_ref
  1.9 0.2 join.1
  2.1 4.3 %collective-permute-start.2 = (bf16[528,128]{1,0:T(8,128)(2,1)S(1)}, bf16[528,128]{1,0:T(8,128)(2,1)S(1)}, u32[]{:S(2)}, u32[]{:S(2)}) collective-permute-start(bf16[528,128]{1,0:T(8,128)(2,1)S(1)} %get-tuple-element.40), channel_id=1, source_target_pairs={{2,6},{8,12},{10,14},{16,20},{18,22},{24,28},{3,5},{7,9},{11,13},{... | collective-permute-start | bytes 405512 | tf_op jit(solution)/shard_map/ppermute | solution.py:506
  6.4 0.0 collective-permute-start.1
  6.4 4.1 %early.1 = (bf16[1024,1792]{1,0:T(8,128)(2,1)S(1)}, bf16[1792,1024]{1,0:T(8,128)(2,1)S(1)}, s32[24,32]{1,0:T(8,128)S(1)}, f32[7,512,128]{2,1,0:T(8,128)S(1)}, f32[7,512,128]{2,1,0:T(8,128)S(1)}) custom-call(bf16[528,128]{1,0:T(8,128)(2,1)S(1)} %get-tuple-element.39.both_ref, bf16[2,1024,896]{2,1,0:T(8,128)(2,1)} %bitcast.7, ...), custom_call_target="tpu_custom_call" | custom-call | flops 1 | bytes 1 | tf_op jit(solution)/shard_map/early/pallas_call | solution.py:547
  10.5 0.4 %collective-permute-done.2.first_ref = bf16[528,128]{1,0:T(8,128)(2,1)S(1)} collective-permute-done((bf16[528,128]{1,0:T(8,128)(2,1)S(1)}, bf16[528,128]{1,0:T(8,128)(2,1)S(1)}, u32[]{:S(2)}, u32[]{:S(2)}) %collective-permute-start.2) | collective-permute-done | bytes 135200 | tf_op jit(solution)/shard_map/ppermute | solution.py:506
  10.9 0.7 %collective-permute-done.1.second_ref = bf16[528,128]{1,0:T(8,128)(2,1)S(1)} collective-permute-done((bf16[528,128]{1,0:T(8,128)(2,1)S(1)}, bf16[528,128]{1,0:T(8,128)(2,1)S(1)}, u32[]{:S(2)}, u32[]{:S(2)}) %collective-permute-start.1) | collective-permute-done | bytes 135200 | tf_op jit(solution)/shard_map/ppermute | solution.py:506
  11.6 0.9 %collective-permute-start.3 = (bf16[1056,128]{1,0:T(8,128)(2,1)S(1)}, bf16[1056,128]{1,0:T(8,128)(2,1)S(1)}, u32[]{:S(2)}, u32[]{:S(2)}) collective-permute-start(bf16[1056,128]{1,0:T(8,128)(2,1)S(1)} %pad_maximum_fusion), channel_id=1, source_target_pairs={{0,1},{1,0},{2,3},{3,2},{4,5},{5,4},{6,7},{7,6},{8,9},{9,8},{10,11... | collective-permute-start | bytes 811016 | tf_op jit(solution)/shard_map/ppermute | solution.py:506
  12.5 0.8 %middle.1.begun_ref = f32[7,512,128]{2,1,0:T(8,128)S(1)} custom-call(s32[24,32]{1,0:T(8,128)S(1)} %get-tuple-element.46.lists_ref, bf16[528,128]{1,0:T(8,128)(2,1)S(1)} %collective-permute-done.2.first_ref, bf16[528,128]{1,0:T(8,128)(2,1)S(1)} %collective-permute-done.1.second_ref, bf16[1024,1792]{1,0:T(8,128)(2,1)S(1)} %get-tuple-element.49.table_ref, ...), custom_call_target="tpu_custom_call" | custom-call | flops 1 | bytes 1 | tf_op jit(solution)/shard_map/middle/pallas_call | solution.py:606
  13.3 0.4 %collective-permute-done.3.far_ref = bf16[1056,128]{1,0:T(8,128)(2,1)S(1)} collective-permute-done((bf16[1056,128]{1,0:T(8,128)(2,1)S(1)}, bf16[1056,128]{1,0:T(8,128)(2,1)S(1)}, u32[]{:S(2)}, u32[]{:S(2)}) %collective-permute-start.3) | collective-permute-done | bytes 270368 | tf_op jit(solution)/shard_map/ppermute | solution.py:506
  13.7 2.1 %main.1 = (f32[7,512,128]{2,1,0:T(8,128)S(1)}, f32[128,1024]{1,0:T(8,128)S(1)}) custom-call(s32[24,32]{1,0:T(8,128)S(1)} %get-tuple-element.46.lists_ref, bf16[1056,128]{1,0:T(8,128)(2,1)S(1)} %collective-permute-done.3.far_ref, bf16[1024,1792]{1,0:T(8,128)(2,1)S(1)} %get-tuple-element.49.table_ref, bf16[1792,1024]{1,0:T(8,128)(2,1)S(1)} %get-tuple-element.52.turned_ref, ...), custom_call_target="tpu_custom_call" | custom-call | flops 1 | bytes 1 | tf_op jit(solution)/shard_map/main/pallas_call | solution.py:617
  15.8 0.2 collective-permute-start.4
  15.9 1.5 %rest.1 = f32[128,1024]{1,0:T(8,128)S(1)} custom-call(s32[24,32]{1,0:T(8,128)S(1)} %get-tuple-element.46.lists_ref, bf16[1792,1024]{1,0:T(8,128)(2,1)S(1)} %get-tuple-element.52.turned_ref, f32[7,512,128]{2,1,0:T(8,128)S(1)} %get-tuple-element.56.sino_ref, f32[7,512,128]{2,1,0:T(8,128)S(1)} %get-tuple-element.54.decay_ref), custom_call_target="tpu_custom_call" | custom-call | flops 1 | bytes 1 | tf_op jit(solution)/shard_map/rest/pallas_call | solution.py:628
  17.4 0.3 %collective-permute-done.4 = f32[128,1024]{1,0:T(8,128)S(1)} collective-permute-done((f32[128,1024]{1,0:T(8,128)S(1)}, f32[128,1024]{1,0:T(8,128)S(1)}, u32[]{:S(2)}, u32[]{:S(2)}) %collective-permute-start.4) | collective-permute-done | bytes 524320 | tf_op jit(solution)/shard_map/ppermute | solution.py:506
  17.8 0.1 add_convert_fusion
  17.8 2.9 %collective-permute-start.6 = (bf16[64,1024]{1,0:T(8,128)(2,1)S(1)}, bf16[64,1024]{1,0:T(8,128)(2,1)S(1)}, u32[]{:S(2)}, u32[]{:S(2)}) collective-permute-start(bf16[64,1024]{1,0:T(8,128)(2,1)S(1)} %get-tuple-element.63), channel_id=1, source_target_pairs={{6,2},{12,8},{14,10},{20,16},{22,18},{28,24},{5,3},{9,7},{13,11},{... | collective-permute-start | bytes 393224 | tf_op jit(solution)/shard_map/ppermute | solution.py:506
  20.7 0.0 collective-permute-start.5
  20.7 0.2 prior.1.prior_ref
  20.9 1.4 %home.1 = f32[64,1024]{1,0:T(8,128)S(1)} custom-call(s32[24,32]{1,0:T(8,128)S(1)} %get-tuple-element.46.lists_ref, bf16[1792,1024]{1,0:T(8,128)(2,1)S(1)} %get-tuple-element.52.turned_ref, f32[7,512,128]{2,1,0:T(8,128)S(1)} %get-tuple-element.56.sino_ref, f32[7,512,128]{2,1,0:T(8,128)S(1)} %get-tuple-element.54.decay_ref), custom_call_target="tpu_custom_call" | custom-call | flops 1 | bytes 1 | tf_op jit(solution)/shard_map/home/pallas_call | solution.py:643
  22.3 3.7 %collective-permute-done.6 = bf16[64,1024]{1,0:T(8,128)(2,1)S(1)} collective-permute-done((bf16[64,1024]{1,0:T(8,128)(2,1)S(1)}, bf16[64,1024]{1,0:T(8,128)(2,1)S(1)}, u32[]{:S(2)}, u32[]{:S(2)}) %collective-permute-start.6) | collective-permute-done | bytes 131104 | tf_op jit(solution)/shard_map/ppermute | solution.py:506
  26.0 0.0 collective-permute-done.5
  26.1 0.5 %collective-permute-start.7 = (f32[32,1024]{1,0:T(8,128)S(1)}, f32[32,1024]{1,0:T(8,128)S(1)}, u32[]{:S(2)}, u32[]{:S(2)}) collective-permute-start(f32[32,1024]{1,0:T(8,128)S(1)} %get-tuple-element.65), channel_id=1, source_target_pairs={{0,1},{1,0},{2,3},{3,2},{4,5},{5,4},{6,7},{7,6},{8,9},{9,8},{10,11... | collective-permute-start | bytes 393224 | tf_op jit(solution)/shard_map/ppermute | solution.py:506
  26.5 1.0 %collective-permute-done.7.passed_ref = f32[32,1024]{1,0:T(8,128)S(1)} collective-permute-done((f32[32,1024]{1,0:T(8,128)S(1)}, f32[32,1024]{1,0:T(8,128)S(1)}, u32[]{:S(2)}, u32[]{:S(2)}) %collective-permute-start.7) | collective-permute-done | bytes 131104 | tf_op jit(solution)/shard_map/ppermute | solution.py:506
  27.5 0.7 %last.1 = f32[32,2,512]{2,1,0:T(2,128)} custom-call(f32[32,1024]{1,0:T(8,128)S(1)} %get-tuple-element.66.arrived_ref, f32[32,1024]{1,0:T(8,128)S(1)} %collective-permute-done.7.passed_ref, f32[32,1024]{1,0:T(8,128)S(1)} %prior.1.prior_ref), custom_call_target="tpu_custom_call" | custom-call | tf_op jit(solution)/shard_map/last/pallas_call | solution.py:670
  (2 shorter events, 0.1 us)
Async XLA Ops:
  0.0 1.9 %collective-permute-start = (f32[32,2,512]{2,1,0:T(2,128)}, f32[32,2,512]{2,1,0:T(2,128)S(1)}, u32[]{:S(2)}, u32[]{:S(2)}) collective-permute-start(f32[32,2,512]{2,1,0:T(2,128)} %bitcast.8), channel_id=1, source_target_pairs={{0,1},{1,0},{2,3},{3,2},{4,5},{5,4},{6,7},{7,6},{8,9},{9,8},{10,11... | collective-permute-start | bytes 393224 | tf_op jit(solution)/shard_map/ppermute | solution.py:506
  2.1 8.8 %collective-permute-start.2 = (bf16[528,128]{1,0:T(8,128)(2,1)S(1)}, bf16[528,128]{1,0:T(8,128)(2,1)S(1)}, u32[]{:S(2)}, u32[]{:S(2)}) collective-permute-start(bf16[528,128]{1,0:T(8,128)(2,1)S(1)} %get-tuple-element.40), channel_id=1, source_target_pairs={{2,6},{8,12},{10,14},{16,20},{18,22},{24,28},{3,5},{7,9},{11,13},{... | collective-permute-start | bytes 405512 | tf_op jit(solution)/shard_map/ppermute | solution.py:506
  6.4 5.2 %collective-permute-start.1 = (bf16[528,128]{1,0:T(8,128)(2,1)S(1)}, bf16[528,128]{1,0:T(8,128)(2,1)S(1)}, u32[]{:S(2)}, u32[]{:S(2)}) collective-permute-start(bf16[528,128]{1,0:T(8,128)(2,1)S(1)} %get-tuple-element.39.both_ref), channel_id=1, source_target_pairs={{4,8},{6,10},{12,16},{14,18},{20,24},{22,26},{0,2},{28,30},{1,3},{... | collective-permute-start | bytes 405512 | tf_op jit(solution)/shard_map/ppermute | solution.py:506
  11.6 2.1 %collective-permute-start.3 = (bf16[1056,128]{1,0:T(8,128)(2,1)S(1)}, bf16[1056,128]{1,0:T(8,128)(2,1)S(1)}, u32[]{:S(2)}, u32[]{:S(2)}) collective-permute-start(bf16[1056,128]{1,0:T(8,128)(2,1)S(1)} %pad_maximum_fusion), channel_id=1, source_target_pairs={{0,1},{1,0},{2,3},{3,2},{4,5},{5,4},{6,7},{7,6},{8,9},{9,8},{10,11... | collective-permute-start | bytes 811016 | tf_op jit(solution)/shard_map/ppermute | solution.py:506
  15.8 2.0 %collective-permute-start.4 = (f32[128,1024]{1,0:T(8,128)S(1)}, f32[128,1024]{1,0:T(8,128)S(1)}, u32[]{:S(2)}, u32[]{:S(2)}) collective-permute-start(f32[128,1024]{1,0:T(8,128)S(1)} %get-tuple-element.55), channel_id=1, source_target_pairs={{0,1},{1,0},{2,3},{3,2},{4,5},{5,4},{6,7},{7,6},{8,9},{9,8},{10,11... | collective-permute-start | bytes 1572872 | tf_op jit(solution)/shard_map/ppermute | solution.py:506
  17.8 8.1 %collective-permute-start.6 = (bf16[64,1024]{1,0:T(8,128)(2,1)S(1)}, bf16[64,1024]{1,0:T(8,128)(2,1)S(1)}, u32[]{:S(2)}, u32[]{:S(2)}) collective-permute-start(bf16[64,1024]{1,0:T(8,128)(2,1)S(1)} %get-tuple-element.63), channel_id=1, source_target_pairs={{6,2},{12,8},{14,10},{20,16},{22,18},{28,24},{5,3},{9,7},{13,11},{... | collective-permute-start | bytes 393224 | tf_op jit(solution)/shard_map/ppermute | solution.py:506
  20.7 5.3 %collective-permute-start.5 = (bf16[64,1024]{1,0:T(8,128)(2,1)S(1)}, bf16[64,1024]{1,0:T(8,128)(2,1)S(1)}, u32[]{:S(2)}, u32[]{:S(2)}) collective-permute-start(bf16[64,1024]{1,0:T(8,128)(2,1)S(1)} %get-tuple-element.64), channel_id=1, source_target_pairs={{8,4},{10,6},{16,12},{18,14},{24,20},{26,22},{2,0},{30,28},{3,1},{... | collective-permute-start | bytes 393224 | tf_op jit(solution)/shard_map/ppermute | solution.py:506
  26.1 1.4 %collective-permute-start.7 = (f32[32,1024]{1,0:T(8,128)S(1)}, f32[32,1024]{1,0:T(8,128)S(1)}, u32[]{:S(2)}, u32[]{:S(2)}) collective-permute-start(f32[32,1024]{1,0:T(8,128)S(1)} %get-tuple-element.65), channel_id=1, source_target_pairs={{0,1},{1,0},{2,3},{3,2},{4,5},{5,4},{6,7},{7,6},{8,9},{9,8},{10,11... | collective-permute-start | bytes 393224 | tf_op jit(solution)/shard_map/ppermute | solution.py:506

commit v3 on v2

--- a/solution.py
+++ b/solution.py
@@ -320,6 +320,9 @@
     index[2 * slots : 2 * slots + 1, :] = count[...]
     index[2 * slots + 1 : 2 * slots + 2, :] = angle[...]
     load = fetch(index, scal, sems.at[0])
+    load.wait()
+    list_pairs(scal, lists, seen, height, held, 2 * piece, det_rows, tables, slab)
+    save = fetch(lists, lists_ref, sems.at[0])
     copies[4].wait()
 
     def fade(view, carry):
@@ -331,9 +334,6 @@
         return carry
 
     lax.fori_loop(0, views, fade, 0)
-    load.wait()
-    list_pairs(scal, lists, seen, height, held, 2 * piece, det_rows, tables, slab)
-    save = fetch(lists, lists_ref, sems.at[0])
     for copy in copies[5:]:
         copy.wait()
     proj[...] = jnp.dot(window[...], table_ref[...], preferred_element_type=jnp.float32)

time: 28.5 us -> 28.4 us (level)
  waiting for transfers between devices: 6.62 us -> 6.22 us
    ppermute x8, waiting for transfers between devices: 6.62 us -> 6.22 us  [shards(): send = lambda value, pairs: lax.ppermute(value, AXES, pairs)]
  transfers between devices with their start and end apart: 8 -> 8, of which waited for: 7 -> 8; matrix products, arithmetic and copies ran while one was open for 0% -> 0% of each run, Pallas kernels for 32% -> 33%
where the time goes in v3:
time: 28.4 us; the launch traced here: 28 us
  Pallas kernels  12.1 us (43%)
  starting transfers between devices  9.54 us (34%)
  waiting for transfers between devices  6.22 us (22%)
    ppermute x8, starting transfers between devices, shards(): send = lambda value, pairs: lax.ppermute(value, AXES, pairs)  9.54 us
    ppermute x8, waiting for transfers between devices, shards(): send = lambda value, pairs: lax.ppermute(value, AXES, pairs)  6.22 us
    pallas_call x1, Pallas kernels, shards(): pl.pallas_call(functools.partial(early_kernel, piece=piece, chips=devices...  4.2 us
    pallas_call x1, Pallas kernels, shards(): pl.pallas_call(functools.partial(main_kernel, slab=slab), out_shape=(sino...  1.88 us
    pallas_call x1, Pallas kernels, shards(): pl.pallas_call(functools.partial(rest_kernel, group=0, slab=slab), out_sh...  1.6 us
    pallas_call x1, Pallas kernels, shards(): pl.pallas_call(functools.partial(rest_kernel, group=2, slab=slab), out_sh...  1.38 us
    pallas_call x1, Pallas kernels, shards(): pl.pallas_call(load_kernel, out_shape=(shape(flat.shape, flat.dtype), sha...  1.04 us
    pallas_call x1, Pallas kernels, shards(): pl.pallas_call(functools.partial(middle_kernel, slab=slab), out_shape=sin...  0.87 us
  transfers between devices with their start and end apart: 8, of which 8 were waited for; matrix products, arithmetic and copies ran while one was open for 0% of the time, Pallas kernels for 33%

profile of v3, /device:TPU:3, one launch (start us, length us, event | category | flops | bytes accessed | tf_op | source)
XLA Modules:
  0.0 28.0 jit_solution(16416457864268158861)
XLA Ops:
  0.0 0.7 %collective-permute-start = (f32[32,2,512]{2,1,0:T(2,128)}, f32[32,2,512]{2,1,0:T(2,128)S(1)}, u32[]{:S(2)}, u32[]{:S(2)}) collective-permute-start(f32[32,2,512]{2,1,0:T(2,128)} %bitcast.8), channel_id=1, source_target_pairs={{0,1},{1,0},{2,3},{3,2},{4,5},{5,4},{6,7},{7,6},{8,9},{9,8},{10,11... | collective-permute-start | bytes 393224 | tf_op jit(solution)/shard_map/ppermute | solution.py:506
  0.7 1.0 %load.1 = (f32[32,2,512]{2,1,0:T(2,128)S(1)}, bf16[32,1024]{1,0:T(8,128)(2,1)S(1)}) custom-call(f32[32,2,512]{2,1,0:T(2,128)} %bitcast.9), custom_call_target="tpu_custom_call" | custom-call | flops 1 | bytes 1 | tf_op jit(solution)/shard_map/load/pallas_call | solution.py:522
  1.7 0.1 collective-permute-done.other_ref
  1.9 0.2 join.1
  2.1 4.3 %collective-permute-start.2 = (bf16[528,128]{1,0:T(8,128)(2,1)S(1)}, bf16[528,128]{1,0:T(8,128)(2,1)S(1)}, u32[]{:S(2)}, u32[]{:S(2)}) collective-permute-start(bf16[528,128]{1,0:T(8,128)(2,1)S(1)} %get-tuple-element.40), channel_id=1, source_target_pairs={{2,6},{8,12},{10,14},{16,20},{18,22},{24,28},{3,5},{7,9},{11,13},{... | collective-permute-start | bytes 405512 | tf_op jit(solution)/shard_map/ppermute | solution.py:506
  6.4 0.0 collective-permute-start.1
  6.4 4.2 %early.1 = (bf16[1024,1792]{1,0:T(8,128)(2,1)S(1)}, bf16[1792,1024]{1,0:T(8,128)(2,1)S(1)}, s32[24,32]{1,0:T(8,128)S(1)}, f32[7,512,128]{2,1,0:T(8,128)S(1)}, f32[7,512,128]{2,1,0:T(8,128)S(1)}) custom-call(bf16[528,128]{1,0:T(8,128)(2,1)S(1)} %get-tuple-element.39.both_ref, bf16[2,1024,896]{2,1,0:T(8,128)(2,1)} %bitcast.7, ...), custom_call_target="tpu_custom_call" | custom-call | flops 1 | bytes 1 | tf_op jit(solution)/shard_map/early/pallas_call | solution.py:547
  10.6 0.3 collective-permute-done.2.first_ref
  10.9 0.7 %collective-permute-done.1.second_ref = bf16[528,128]{1,0:T(8,128)(2,1)S(1)} collective-permute-done((bf16[528,128]{1,0:T(8,128)(2,1)S(1)}, bf16[528,128]{1,0:T(8,128)(2,1)S(1)}, u32[]{:S(2)}, u32[]{:S(2)}) %collective-permute-start.1) | collective-permute-done | bytes 135200 | tf_op jit(solution)/shard_map/ppermute | solution.py:506
  11.6 0.9 %collective-permute-start.3 = (bf16[1056,128]{1,0:T(8,128)(2,1)S(1)}, bf16[1056,128]{1,0:T(8,128)(2,1)S(1)}, u32[]{:S(2)}, u32[]{:S(2)}) collective-permute-start(bf16[1056,128]{1,0:T(8,128)(2,1)S(1)} %pad_maximum_fusion), channel_id=1, source_target_pairs={{0,1},{1,0},{2,3},{3,2},{4,5},{5,4},{6,7},{7,6},{8,9},{9,8},{10,11... | collective-permute-start | bytes 811016 | tf_op jit(solution)/shard_map/ppermute | solution.py:506
  12.5 0.9 %middle.1.begun_ref = f32[7,512,128]{2,1,0:T(8,128)S(1)} custom-call(s32[24,32]{1,0:T(8,128)S(1)} %get-tuple-element.46.lists_ref, bf16[528,128]{1,0:T(8,128)(2,1)S(1)} %collective-permute-done.2.first_ref, bf16[528,128]{1,0:T(8,128)(2,1)S(1)} %collective-permute-done.1.second_ref, bf16[1024,1792]{1,0:T(8,128)(2,1)S(1)} %get-tuple-element.49.table_ref, ...), custom_call_target="tpu_custom_call" | custom-call | flops 1 | bytes 1 | tf_op jit(solution)/shard_map/middle/pallas_call | solution.py:606
  13.4 0.3 %collective-permute-done.3.far_ref = bf16[1056,128]{1,0:T(8,128)(2,1)S(1)} collective-permute-done((bf16[1056,128]{1,0:T(8,128)(2,1)S(1)}, bf16[1056,128]{1,0:T(8,128)(2,1)S(1)}, u32[]{:S(2)}, u32[]{:S(2)}) %collective-permute-start.3) | collective-permute-done | bytes 270368 | tf_op jit(solution)/shard_map/ppermute | solution.py:506
  13.7 1.9 %main.1 = (f32[7,512,128]{2,1,0:T(8,128)S(1)}, f32[128,1024]{1,0:T(8,128)S(1)}) custom-call(s32[24,32]{1,0:T(8,128)S(1)} %get-tuple-element.46.lists_ref, bf16[1056,128]{1,0:T(8,128)(2,1)S(1)} %collective-permute-done.3.far_ref, bf16[1024,1792]{1,0:T(8,128)(2,1)S(1)} %get-tuple-element.49.table_ref, bf16[1792,1024]{1,0:T(8,128)(2,1)S(1)} %get-tuple-element.52.turned_ref, ...), custom_call_target="tpu_custom_call" | custom-call | flops 1 | bytes 1 | tf_op jit(solution)/shard_map/main/pallas_call | solution.py:617
  15.5 0.2 collective-permute-start.4
  15.7 1.6 %rest.1 = f32[128,1024]{1,0:T(8,128)S(1)} custom-call(s32[24,32]{1,0:T(8,128)S(1)} %get-tuple-element.46.lists_ref, bf16[1792,1024]{1,0:T(8,128)(2,1)S(1)} %get-tuple-element.52.turned_ref, f32[7,512,128]{2,1,0:T(8,128)S(1)} %get-tuple-element.56.sino_ref, f32[7,512,128]{2,1,0:T(8,128)S(1)} %get-tuple-element.54.decay_ref), custom_call_target="tpu_custom_call" | custom-call | flops 1 | bytes 1 | tf_op jit(solution)/shard_map/rest/pallas_call | solution.py:628
  17.3 0.2 collective-permute-done.4
  17.5 0.1 add_convert_fusion
  17.6 3.1 %collective-permute-start.6 = (bf16[64,1024]{1,0:T(8,128)(2,1)S(1)}, bf16[64,1024]{1,0:T(8,128)(2,1)S(1)}, u32[]{:S(2)}, u32[]{:S(2)}) collective-permute-start(bf16[64,1024]{1,0:T(8,128)(2,1)S(1)} %get-tuple-element.63), channel_id=1, source_target_pairs={{6,2},{12,8},{14,10},{20,16},{22,18},{28,24},{5,3},{9,7},{13,11},{... | collective-permute-start | bytes 393224 | tf_op jit(solution)/shard_map/ppermute | solution.py:506
  20.6 0.0 collective-permute-start.5
  20.6 0.2 prior.1.prior_ref
  20.8 1.4 %home.1 = f32[64,1024]{1,0:T(8,128)S(1)} custom-call(s32[24,32]{1,0:T(8,128)S(1)} %get-tuple-element.46.lists_ref, bf16[1792,1024]{1,0:T(8,128)(2,1)S(1)} %get-tuple-element.52.turned_ref, f32[7,512,128]{2,1,0:T(8,128)S(1)} %get-tuple-element.56.sino_ref, f32[7,512,128]{2,1,0:T(8,128)S(1)} %get-tuple-element.54.decay_ref), custom_call_target="tpu_custom_call" | custom-call | flops 1 | bytes 1 | tf_op jit(solution)/shard_map/home/pallas_call | solution.py:643
  22.2 3.0 %collective-permute-done.6 = bf16[64,1024]{1,0:T(8,128)(2,1)S(1)} collective-permute-done((bf16[64,1024]{1,0:T(8,128)(2,1)S(1)}, bf16[64,1024]{1,0:T(8,128)(2,1)S(1)}, u32[]{:S(2)}, u32[]{:S(2)}) %collective-permute-start.6) | collective-permute-done | bytes 131104 | tf_op jit(solution)/shard_map/ppermute | solution.py:506
  25.3 0.6 %collective-permute-done.5 = bf16[64,1024]{1,0:T(8,128)(2,1)S(1)} collective-permute-done((bf16[64,1024]{1,0:T(8,128)(2,1)S(1)}, bf16[64,1024]{1,0:T(8,128)(2,1)S(1)}, u32[]{:S(2)}, u32[]{:S(2)}) %collective-permute-start.5) | collective-permute-done | bytes 131104 | tf_op jit(solution)/shard_map/ppermute | solution.py:506
  25.9 0.4 %collective-permute-start.7 = (f32[32,1024]{1,0:T(8,128)S(1)}, f32[32,1024]{1,0:T(8,128)S(1)}, u32[]{:S(2)}, u32[]{:S(2)}) collective-permute-start(f32[32,1024]{1,0:T(8,128)S(1)} %get-tuple-element.65), channel_id=1, source_target_pairs={{0,1},{1,0},{2,3},{3,2},{4,5},{5,4},{6,7},{7,6},{8,9},{9,8},{10,11... | collective-permute-start | bytes 393224 | tf_op jit(solution)/shard_map/ppermute | solution.py:506
  26.3 1.0 %collective-permute-done.7.passed_ref = f32[32,1024]{1,0:T(8,128)S(1)} collective-permute-done((f32[32,1024]{1,0:T(8,128)S(1)}, f32[32,1024]{1,0:T(8,128)S(1)}, u32[]{:S(2)}, u32[]{:S(2)}) %collective-permute-start.7) | collective-permute-done | bytes 131104 | tf_op jit(solution)/shard_map/ppermute | solution.py:506
  27.3 0.7 %last.1 = f32[32,2,512]{2,1,0:T(2,128)} custom-call(f32[32,1024]{1,0:T(8,128)S(1)} %get-tuple-element.66.arrived_ref, f32[32,1024]{1,0:T(8,128)S(1)} %collective-permute-done.7.passed_ref, f32[32,1024]{1,0:T(8,128)S(1)} %prior.1.prior_ref), custom_call_target="tpu_custom_call" | custom-call | tf_op jit(solution)/shard_map/last/pallas_call | solution.py:670
  (2 shorter events, 0.1 us)
Async XLA Ops:
  0.0 1.9 %collective-permute-start = (f32[32,2,512]{2,1,0:T(2,128)}, f32[32,2,512]{2,1,0:T(2,128)S(1)}, u32[]{:S(2)}, u32[]{:S(2)}) collective-permute-start(f32[32,2,512]{2,1,0:T(2,128)} %bitcast.8), channel_id=1, source_target_pairs={{0,1},{1,0},{2,3},{3,2},{4,5},{5,4},{6,7},{7,6},{8,9},{9,8},{10,11... | collective-permute-start | bytes 393224 | tf_op jit(solution)/shard_map/ppermute | solution.py:506
  2.1 8.8 %collective-permute-start.2 = (bf16[528,128]{1,0:T(8,128)(2,1)S(1)}, bf16[528,128]{1,0:T(8,128)(2,1)S(1)}, u32[]{:S(2)}, u32[]{:S(2)}) collective-permute-start(bf16[528,128]{1,0:T(8,128)(2,1)S(1)} %get-tuple-element.40), channel_id=1, source_target_pairs={{2,6},{8,12},{10,14},{16,20},{18,22},{24,28},{3,5},{7,9},{11,13},{... | collective-permute-start | bytes 405512 | tf_op jit(solution)/shard_map/ppermute | solution.py:506
  6.4 5.2 %collective-permute-start.1 = (bf16[528,128]{1,0:T(8,128)(2,1)S(1)}, bf16[528,128]{1,0:T(8,128)(2,1)S(1)}, u32[]{:S(2)}, u32[]{:S(2)}) collective-permute-start(bf16[528,128]{1,0:T(8,128)(2,1)S(1)} %get-tuple-element.39.both_ref), channel_id=1, source_target_pairs={{4,8},{6,10},{12,16},{14,18},{20,24},{22,26},{0,2},{28,30},{1,3},{... | collective-permute-start | bytes 405512 | tf_op jit(solution)/shard_map/ppermute | solution.py:506
  11.6 2.1 %collective-permute-start.3 = (bf16[1056,128]{1,0:T(8,128)(2,1)S(1)}, bf16[1056,128]{1,0:T(8,128)(2,1)S(1)}, u32[]{:S(2)}, u32[]{:S(2)}) collective-permute-start(bf16[1056,128]{1,0:T(8,128)(2,1)S(1)} %pad_maximum_fusion), channel_id=1, source_target_pairs={{0,1},{1,0},{2,3},{3,2},{4,5},{5,4},{6,7},{7,6},{8,9},{9,8},{10,11... | collective-permute-start | bytes 811016 | tf_op jit(solution)/shard_map/ppermute | solution.py:506
  15.5 2.0 %collective-permute-start.4 = (f32[128,1024]{1,0:T(8,128)S(1)}, f32[128,1024]{1,0:T(8,128)S(1)}, u32[]{:S(2)}, u32[]{:S(2)}) collective-permute-start(f32[128,1024]{1,0:T(8,128)S(1)} %get-tuple-element.55), channel_id=1, source_target_pairs={{0,1},{1,0},{2,3},{3,2},{4,5},{5,4},{6,7},{7,6},{8,9},{9,8},{10,11... | collective-permute-start | bytes 1572872 | tf_op jit(solution)/shard_map/ppermute | solution.py:506
  17.6 7.7 %collective-permute-start.6 = (bf16[64,1024]{1,0:T(8,128)(2,1)S(1)}, bf16[64,1024]{1,0:T(8,128)(2,1)S(1)}, u32[]{:S(2)}, u32[]{:S(2)}) collective-permute-start(bf16[64,1024]{1,0:T(8,128)(2,1)S(1)} %get-tuple-element.63), channel_id=1, source_target_pairs={{6,2},{12,8},{14,10},{20,16},{22,18},{28,24},{5,3},{9,7},{13,11},{... | collective-permute-start | bytes 393224 | tf_op jit(solution)/shard_map/ppermute | solution.py:506
  20.6 5.2 %collective-permute-start.5 = (bf16[64,1024]{1,0:T(8,128)(2,1)S(1)}, bf16[64,1024]{1,0:T(8,128)(2,1)S(1)}, u32[]{:S(2)}, u32[]{:S(2)}) collective-permute-start(bf16[64,1024]{1,0:T(8,128)(2,1)S(1)} %get-tuple-element.64), channel_id=1, source_target_pairs={{8,4},{10,6},{16,12},{18,14},{24,20},{26,22},{2,0},{30,28},{3,1},{... | collective-permute-start | bytes 393224 | tf_op jit(solution)/shard_map/ppermute | solution.py:506
  25.9 1.4 %collective-permute-start.7 = (f32[32,1024]{1,0:T(8,128)S(1)}, f32[32,1024]{1,0:T(8,128)S(1)}, u32[]{:S(2)}, u32[]{:S(2)}) collective-permute-start(f32[32,1024]{1,0:T(8,128)S(1)} %get-tuple-element.65), channel_id=1, source_target_pairs={{0,1},{1,0},{2,3},{3,2},{4,5},{5,4},{6,7},{7,6},{8,9},{9,8},{10,11... | collective-permute-start | bytes 393224 | tf_op jit(solution)/shard_map/ppermute | solution.py:506
